TPU v7x, 512 devices: a whole 4x4x16 slice. The times are simulated.
512 devices in a mesh: tm: 32 (over y_lo, z), space: 16 (over y_hi, x, core).
Axes of the slice: x: 4, y: 4 (y_hi: 2, y_lo: 2; y = y_hi * 2 + y_lo), z: 16, core: 2. Of those that a mesh axis runs over, the one named last changes fastest.
Arguments:
- cstates: float32 [32, 256, 2048], P('tm', 'space'), may hold values from -4 to 4
- drift: float32 [2, 256, 2048], P(None, 'space'), may hold values from -0.2 to 0.2
- diffusivity: float32 [256, 2048], P('space'), may hold values from 0.1 to 0.24
- coarse_rate: float32 [256, 2048], P('space'), may hold values from 0.00625 to 0.625
Outputs:
- cpoints: float32 [32, 256, 2048], P('tm', 'space')
- coarse_residual: float32 [32, 256, 2048], P('tm', 'space')
All inputs are finite; a program needn't handle non-finite values.
Results may differ from a plain program's by a relative error of at most 0.00018.
Values sent between devices are 32-bit elements; how exact they have to be, the bound alone decides.
No kernel may reach another device: no remote copies, remote signals or barrier semaphores. Data moves between devices by JAX's collectives and lax.ppermute only.
A program may use at most 64 MiB of HBM per device.

v0:
```python
import jax
import jax.numpy as jnp
from jax import lax
from jax.sharding import PartitionSpec as P

M = 8


nonlinear_weight = 0.05


def with_halo(cells, sides, width):
    for axis, dim in sides:
        count = lax.axis_size(axis)
        head = lax.slice_in_dim(cells, 0, width, axis=dim)
        tail = lax.slice_in_dim(cells, cells.shape[dim] - width, cells.shape[dim], axis=dim)
        cells = jnp.concatenate(
            [
                lax.ppermute(tail, axis, [(i, (i + 1) % count) for i in range(count)]),
                cells,
                lax.ppermute(head, axis, [((i + 1) % count, i) for i in range(count)]),
            ],
            axis=dim,
        )
    return cells


def passed_along(value, axis, steps):
    count = lax.axis_size(axis)
    pairs = [(source, (source + steps) % count) for source in range(count)]
    return lax.ppermute(value, axis, pairs)


def advance_rows(extended, drift, diffusivity):
    center = extended[:, 1:-1]
    above = extended[:, 2:]
    below = extended[:, :-2]
    right_cell = jnp.roll(center, -1, axis=2)
    left_cell = jnp.roll(center, 1, axis=2)
    laplacian = above + below + right_cell + left_cell - 4.0 * center
    transport = (drift[0] + nonlinear_weight * center) * (right_cell - left_cell) * 0.5 + drift[
        1
    ] * (above - below) * 0.5
    return center + diffusivity * laplacian - transport


def shards(cstates, drift, diffusivity, coarse_rate):

    def propagate(field):
        for count in range(M):
            extended = with_halo(field, (("space", 1),), 1)
            field = advance_rows(extended, drift, diffusivity)
        return field

    first = propagate(cstates)
    relaxed = passed_along(first, "tm", 1)
    second = propagate(relaxed)
    coarse_residual = passed_along(second, "tm", 1) - relaxed
    decay = jnp.exp(-coarse_rate)[None]
    intervals = lax.axis_size("tm")
    residuals = lax.all_gather(coarse_residual, "tm", axis=0, tiled=True)
    factor = decay[0]

    def accumulate(carry, term):
        following = factor * carry + term
        return (following, following)

    closing, unused = lax.scan(accumulate, jnp.zeros_like(factor), residuals)
    last_error = closing / (1.0 - factor**intervals)
    unused_last, sequence = lax.scan(accumulate, last_error, residuals)
    errors = lax.dynamic_index_in_dim(sequence, lax.axis_index("tm"), 0, keepdims=True)
    cpoints = relaxed + errors
    return (cpoints, coarse_residual)


def solution(mesh):
    placed = (P("tm", "space", None), P(None, "space", None), P("space", None), P("space", None))
    return jax.shard_map(
        shards,
        mesh=mesh,
        in_specs=placed,
        out_specs=(P("tm", "space", None), P("tm", "space", None)),
        check_vma=False,
    )
```

profile of v0, /device:TPU:6, one launch (start us, length us, event | category | flops | bytes accessed | tf_op | source)
XLA Modules:
  0.0 437.3 jit_solution(1389706185105562439)
XLA Ops:
  8.2 2.2 collective-permute-start
  10.4 2.2 collective-permute-start.1
  16.8 2.5 collective-permute-start.2
  19.3 5.1 %collective-permute-start.3 = (f32[1,1,2048]{2,1,0:T(1,128)S(1)}, f32[1,1,2048]{2,1,0:T(1,128)S(1)}, u32[]{:S(2)}, u32[]{:S(2)}) collective-permute-start(f32[1,1,2048]{2,1,0:T(1,128)S(1)} %get-tuple-element.172), channel_id=1, source_target_pairs={{0,1},{1,2},{2,3},{3,4},{4,5},{5,6},{6,7},{7,8},{8,9},{9,10},{10,1... | collective-permute-start | bytes 24584 | tf_op jit(solution)/shard_map/ppermute | solution.py:19
  26.5 1.9 collective-permute-start.4
  28.4 7.2 %collective-permute-start.5 = (f32[1,1,2048]{2,1,0:T(1,128)S(1)}, f32[1,1,2048]{2,1,0:T(1,128)S(1)}, u32[]{:S(2)}, u32[]{:S(2)}) collective-permute-start(f32[1,1,2048]{2,1,0:T(1,128)S(1)} %get-tuple-element.166), channel_id=1, source_target_pairs={{0,1},{1,2},{2,3},{3,4},{4,5},{5,6},{6,7},{7,8},{8,9},{9,10},{10,1... | collective-permute-start | bytes 24584 | tf_op jit(solution)/shard_map/ppermute | solution.py:19
  37.7 1.9 collective-permute-start.6
  39.7 7.8 %collective-permute-start.7 = (f32[1,1,2048]{2,1,0:T(1,128)S(1)}, f32[1,1,2048]{2,1,0:T(1,128)S(1)}, u32[]{:S(2)}, u32[]{:S(2)}) collective-permute-start(f32[1,1,2048]{2,1,0:T(1,128)S(1)} %get-tuple-element.160), channel_id=1, source_target_pairs={{0,1},{1,2},{2,3},{3,4},{4,5},{5,6},{6,7},{7,8},{8,9},{9,10},{10,1... | collective-permute-start | bytes 24584 | tf_op jit(solution)/shard_map/ppermute | solution.py:19
  48.5 1.9 collective-permute-start.8
  50.4 7.8 %collective-permute-start.9 = (f32[1,1,2048]{2,1,0:T(1,128)S(1)}, f32[1,1,2048]{2,1,0:T(1,128)S(1)}, u32[]{:S(2)}, u32[]{:S(2)}) collective-permute-start(f32[1,1,2048]{2,1,0:T(1,128)S(1)} %get-tuple-element.154), channel_id=1, source_target_pairs={{0,1},{1,2},{2,3},{3,4},{4,5},{5,6},{6,7},{7,8},{8,9},{9,10},{10,1... | collective-permute-start | bytes 24584 | tf_op jit(solution)/shard_map/ppermute | solution.py:19
  59.3 1.9 collective-permute-start.10
  61.2 7.8 %collective-permute-start.11 = (f32[1,1,2048]{2,1,0:T(1,128)S(1)}, f32[1,1,2048]{2,1,0:T(1,128)S(1)}, u32[]{:S(2)}, u32[]{:S(2)}) collective-permute-start(f32[1,1,2048]{2,1,0:T(1,128)S(1)} %get-tuple-element.148), channel_id=1, source_target_pairs={{0,1},{1,2},{2,3},{3,4},{4,5},{5,6},{6,7},{7,8},{8,9},{9,10},{10,1... | collective-permute-start | bytes 24584 | tf_op jit(solution)/shard_map/ppermute | solution.py:19
  70.1 1.9 collective-permute-start.12
  72.0 7.8 %collective-permute-start.13 = (f32[1,1,2048]{2,1,0:T(1,128)S(1)}, f32[1,1,2048]{2,1,0:T(1,128)S(1)}, u32[]{:S(2)}, u32[]{:S(2)}) collective-permute-start(f32[1,1,2048]{2,1,0:T(1,128)S(1)} %get-tuple-element.142), channel_id=1, source_target_pairs={{0,1},{1,2},{2,3},{3,4},{4,5},{5,6},{6,7},{7,8},{8,9},{9,10},{10,1... | collective-permute-start | bytes 24584 | tf_op jit(solution)/shard_map/ppermute | solution.py:19
  80.8 1.9 collective-permute-start.14
  82.8 7.8 %collective-permute-start.15 = (f32[1,1,2048]{2,1,0:T(1,128)S(1)}, f32[1,1,2048]{2,1,0:T(1,128)S(1)}, u32[]{:S(2)}, u32[]{:S(2)}) collective-permute-start(f32[1,1,2048]{2,1,0:T(1,128)S(1)} %get-tuple-element.136), channel_id=1, source_target_pairs={{0,1},{1,2},{2,3},{3,4},{4,5},{5,6},{6,7},{7,8},{8,9},{9,10},{10,1... | collective-permute-start | bytes 24584 | tf_op jit(solution)/shard_map/ppermute | solution.py:19
  91.5 3.8 collective-permute-start.16
  95.3 11.5 %collective-permute-done.16 = f32[1,16,2048]{2,1,0:T(8,128)S(1)} collective-permute-done((f32[1,16,2048]{2,1,0:T(8,128)S(1)}, f32[1,16,2048]{2,1,0:T(8,128)S(1)}, u32[]{:S(2)}, u32[]{:S(2)}) %collective-permute-start.16) | collective-permute-done | bytes 131104 | tf_op jit(solution)/shard_map/ppermute | solution.py:31
  106.9 1.9 collective-permute-start.17
  108.8 6.9 %collective-permute-start.18 = (f32[1,1,2048]{2,1,0:T(1,128)S(1)}, f32[1,1,2048]{2,1,0:T(1,128)S(1)}, u32[]{:S(2)}, u32[]{:S(2)}) collective-permute-start(f32[1,1,2048]{2,1,0:T(1,128)S(1)} %get-tuple-element.130), channel_id=1, source_target_pairs={{0,1},{1,2},{2,3},{3,4},{4,5},{5,6},{6,7},{7,8},{8,9},{9,10},{10,1... | collective-permute-start | bytes 24584 | tf_op jit(solution)/shard_map/ppermute | solution.py:19
  118.7 9.2 %collective-permute-start.20 = (f32[1,1,2048]{2,1,0:T(1,128)S(1)}, f32[1,1,2048]{2,1,0:T(1,128)S(1)}, u32[]{:S(2)}, u32[]{:S(2)}) collective-permute-start(f32[1,1,2048]{2,1,0:T(1,128)S(1)} %get-tuple-element.124), channel_id=1, source_target_pairs={{0,1},{1,2},{2,3},{3,4},{4,5},{5,6},{6,7},{7,8},{8,9},{9,10},{10,1... | collective-permute-start | bytes 24584 | tf_op jit(solution)/shard_map/ppermute | solution.py:19
  129.0 1.9 collective-permute-start.21
  130.9 7.8 %collective-permute-start.22 = (f32[1,1,2048]{2,1,0:T(1,128)S(1)}, f32[1,1,2048]{2,1,0:T(1,128)S(1)}, u32[]{:S(2)}, u32[]{:S(2)}) collective-permute-start(f32[1,1,2048]{2,1,0:T(1,128)S(1)} %get-tuple-element.118), channel_id=1, source_target_pairs={{0,1},{1,2},{2,3},{3,4},{4,5},{5,6},{6,7},{7,8},{8,9},{9,10},{10,1... | collective-permute-start | bytes 24584 | tf_op jit(solution)/shard_map/ppermute | solution.py:19
  141.7 7.8 %collective-permute-start.24 = (f32[1,1,2048]{2,1,0:T(1,128)S(1)}, f32[1,1,2048]{2,1,0:T(1,128)S(1)}, u32[]{:S(2)}, u32[]{:S(2)}) collective-permute-start(f32[1,1,2048]{2,1,0:T(1,128)S(1)} %get-tuple-element.112), channel_id=1, source_target_pairs={{0,1},{1,2},{2,3},{3,4},{4,5},{5,6},{6,7},{7,8},{8,9},{9,10},{10,1... | collective-permute-start | bytes 24584 | tf_op jit(solution)/shard_map/ppermute | solution.py:19
  152.5 7.8 %collective-permute-start.26 = (f32[1,1,2048]{2,1,0:T(1,128)S(1)}, f32[1,1,2048]{2,1,0:T(1,128)S(1)}, u32[]{:S(2)}, u32[]{:S(2)}) collective-permute-start(f32[1,1,2048]{2,1,0:T(1,128)S(1)} %get-tuple-element.106), channel_id=1, source_target_pairs={{0,1},{1,2},{2,3},{3,4},{4,5},{5,6},{6,7},{7,8},{8,9},{9,10},{10,1... | collective-permute-start | bytes 24584 | tf_op jit(solution)/shard_map/ppermute | solution.py:19
  163.3 7.8 %collective-permute-start.28 = (f32[1,1,2048]{2,1,0:T(1,128)S(1)}, f32[1,1,2048]{2,1,0:T(1,128)S(1)}, u32[]{:S(2)}, u32[]{:S(2)}) collective-permute-start(f32[1,1,2048]{2,1,0:T(1,128)S(1)} %get-tuple-element.100), channel_id=1, source_target_pairs={{0,1},{1,2},{2,3},{3,4},{4,5},{5,6},{6,7},{7,8},{8,9},{9,10},{10,1... | collective-permute-start | bytes 24584 | tf_op jit(solution)/shard_map/ppermute | solution.py:19
  174.0 7.8 %collective-permute-start.30 = (f32[1,1,2048]{2,1,0:T(1,128)S(1)}, f32[1,1,2048]{2,1,0:T(1,128)S(1)}, u32[]{:S(2)}, u32[]{:S(2)}) collective-permute-start(f32[1,1,2048]{2,1,0:T(1,128)S(1)} %get-tuple-element.94), channel_id=1, source_target_pairs={{0,1},{1,2},{2,3},{3,4},{4,5},{5,6},{6,7},{7,8},{8,9},{9,10},{10,1... | collective-permute-start | bytes 24584 | tf_op jit(solution)/shard_map/ppermute | solution.py:19
  184.8 7.8 %collective-permute-start.32 = (f32[1,1,2048]{2,1,0:T(1,128)S(1)}, f32[1,1,2048]{2,1,0:T(1,128)S(1)}, u32[]{:S(2)}, u32[]{:S(2)}) collective-permute-start(f32[1,1,2048]{2,1,0:T(1,128)S(1)} %get-tuple-element.88), channel_id=1, source_target_pairs={{0,1},{1,2},{2,3},{3,4},{4,5},{5,6},{6,7},{7,8},{8,9},{9,10},{10,1... | collective-permute-start | bytes 24584 | tf_op jit(solution)/shard_map/ppermute | solution.py:19
  195.5 7.0 %collective-permute-done.33 = f32[1,16,2048]{2,1,0:T(8,128)S(1)} collective-permute-done((f32[1,16,2048]{2,1,0:T(8,128)S(1)}, f32[1,16,2048]{2,1,0:T(8,128)S(1)}, u32[]{:S(2)}, u32[]{:S(2)}) %collective-permute-start.33) | collective-permute-done | bytes 131104 | tf_op jit(solution)/shard_map/ppermute | solution.py:31
  203.3 140.8 %all-gather.2.cloned.1.call-done = f32[32,16,2048]{2,1,0:T(8,128)} async-done(((f32[1,16,2048]{2,1,0:T(8,128)}), f32[32,16,2048]{2,1,0:T(8,128)}) %all-gather.2.cloned.1.call-update) | async-done | bytes 4194320 | tf_op jit(solution)/shard_map/all_gather | solution.py:61
  344.0 32.0 %while.24 = (s32[]{:T(128)}, f32[16,2048]{1,0:T(8,128)S(1)}, f32[16,2048]{1,0:T(8,128)S(1)}, f32[32,16,2048]{2,1,0:T(8,128)}, s32[]{:T(128)}, /*index=5*/s32[]{:T(128)}) while((s32[]{:T(128)}, f32[16,2048]{1,0:T(8,128)S(1)}, f32[16,2048]{1,0:T(8,128)S(1)}, f32[32,16,2048]{2,1,0:T(8,128)}, s32[]{:T(128)}, /*index=5*/s32[]{:T(128)}) %tuple.90), condition=%wide.region_1.2_spmd.clone, body=%wide.region_0.1_spmd.clone.sunk | while | flops 98307 | bytes 524371 | solution.py:68
  376.1 52.8 %while.23 = (s32[]{:T(128)}, f32[16,2048]{1,0:T(8,128)S(1)}, f32[32,16,2048]{2,1,0:T(8,128)}, f32[16,2048]{1,0:T(8,128)S(1)}, f32[32,16,2048]{2,1,0:T(8,128)}, /*index=5*/s32[]{:T(128)}) while((s32[]{:T(128)}, f32[16,2048]{1,0:T(8,128)S(1)}, f32[32,16,2048]{2,1,0:T(8,128)}, f32[16,2048]{1,0:T(8,128)S(1)}, f32[32,16,2048]{2,1,0:T(8,128)}, ...), condition=%wide.region_3.4_spmd, body=%wide.region_2.3_spmd.sunk | while | flops 65538 | bytes 655941 | solution.py:70
  (181 shorter events, 122.8 us)
Async XLA Ops:
  7.2 336.8 %all-gather.2.cloned.1.call-start = ((), (), s32[]{:S(2)}) async-start(), calls=%async_computation | async-start | bytes 4325376 | tf_op jit(solution)/shard_map/all_gather | solution.py:61
  16.8 7.7 %collective-permute-start.2 = (f32[1,1,2048]{2,1,0:T(1,128)S(1)}, f32[1,1,2048]{2,1,0:T(1,128)S(1)}, u32[]{:S(2)}, u32[]{:S(2)}) collective-permute-start(f32[1,1,2048]{2,1,0:T(1,128)S(1)} %get-tuple-element.173), channel_id=1, source_target_pairs={{1,0},{2,1},{3,2},{4,3},{5,4},{6,5},{7,6},{8,7},{9,8},{10,9},{11,1... | collective-permute-start | bytes 24584 | tf_op jit(solution)/shard_map/ppermute | solution.py:21
  26.5 9.2 %collective-permute-start.4 = (f32[1,1,2048]{2,1,0:T(1,128)S(1)}, f32[1,1,2048]{2,1,0:T(1,128)S(1)}, u32[]{:S(2)}, u32[]{:S(2)}) collective-permute-start(f32[1,1,2048]{2,1,0:T(1,128)S(1)} %get-tuple-element.167), channel_id=1, source_target_pairs={{1,0},{2,1},{3,2},{4,3},{5,4},{6,5},{7,6},{8,7},{9,8},{10,9},{11,1... | collective-permute-start | bytes 24584 | tf_op jit(solution)/shard_map/ppermute | solution.py:21
  28.4 8.0 %collective-permute-start.5 = (f32[1,1,2048]{2,1,0:T(1,128)S(1)}, f32[1,1,2048]{2,1,0:T(1,128)S(1)}, u32[]{:S(2)}, u32[]{:S(2)}) collective-permute-start(f32[1,1,2048]{2,1,0:T(1,128)S(1)} %get-tuple-element.166), channel_id=1, source_target_pairs={{0,1},{1,2},{2,3},{3,4},{4,5},{5,6},{6,7},{7,8},{8,9},{9,10},{10,1... | collective-permute-start | bytes 24584 | tf_op jit(solution)/shard_map/ppermute | solution.py:19
  37.7 9.8 %collective-permute-start.6 = (f32[1,1,2048]{2,1,0:T(1,128)S(1)}, f32[1,1,2048]{2,1,0:T(1,128)S(1)}, u32[]{:S(2)}, u32[]{:S(2)}) collective-permute-start(f32[1,1,2048]{2,1,0:T(1,128)S(1)} %get-tuple-element.161), channel_id=1, source_target_pairs={{1,0},{2,1},{3,2},{4,3},{5,4},{6,5},{7,6},{8,7},{9,8},{10,9},{11,1... | collective-permute-start | bytes 24584 | tf_op jit(solution)/shard_map/ppermute | solution.py:21
  39.7 8.6 %collective-permute-start.7 = (f32[1,1,2048]{2,1,0:T(1,128)S(1)}, f32[1,1,2048]{2,1,0:T(1,128)S(1)}, u32[]{:S(2)}, u32[]{:S(2)}) collective-permute-start(f32[1,1,2048]{2,1,0:T(1,128)S(1)} %get-tuple-element.160), channel_id=1, source_target_pairs={{0,1},{1,2},{2,3},{3,4},{4,5},{5,6},{6,7},{7,8},{8,9},{9,10},{10,1... | collective-permute-start | bytes 24584 | tf_op jit(solution)/shard_map/ppermute | solution.py:19
  48.5 9.8 %collective-permute-start.8 = (f32[1,1,2048]{2,1,0:T(1,128)S(1)}, f32[1,1,2048]{2,1,0:T(1,128)S(1)}, u32[]{:S(2)}, u32[]{:S(2)}) collective-permute-start(f32[1,1,2048]{2,1,0:T(1,128)S(1)} %get-tuple-element.155), channel_id=1, source_target_pairs={{1,0},{2,1},{3,2},{4,3},{5,4},{6,5},{7,6},{8,7},{9,8},{10,9},{11,1... | collective-permute-start | bytes 24584 | tf_op jit(solution)/shard_map/ppermute | solution.py:21
  50.4 8.6 %collective-permute-start.9 = (f32[1,1,2048]{2,1,0:T(1,128)S(1)}, f32[1,1,2048]{2,1,0:T(1,128)S(1)}, u32[]{:S(2)}, u32[]{:S(2)}) collective-permute-start(f32[1,1,2048]{2,1,0:T(1,128)S(1)} %get-tuple-element.154), channel_id=1, source_target_pairs={{0,1},{1,2},{2,3},{3,4},{4,5},{5,6},{6,7},{7,8},{8,9},{9,10},{10,1... | collective-permute-start | bytes 24584 | tf_op jit(solution)/shard_map/ppermute | solution.py:19
  59.3 9.8 %collective-permute-start.10 = (f32[1,1,2048]{2,1,0:T(1,128)S(1)}, f32[1,1,2048]{2,1,0:T(1,128)S(1)}, u32[]{:S(2)}, u32[]{:S(2)}) collective-permute-start(f32[1,1,2048]{2,1,0:T(1,128)S(1)} %get-tuple-element.149), channel_id=1, source_target_pairs={{1,0},{2,1},{3,2},{4,3},{5,4},{6,5},{7,6},{8,7},{9,8},{10,9},{11,1... | collective-permute-start | bytes 24584 | tf_op jit(solution)/shard_map/ppermute | solution.py:21
  61.2 8.6 %collective-permute-start.11 = (f32[1,1,2048]{2,1,0:T(1,128)S(1)}, f32[1,1,2048]{2,1,0:T(1,128)S(1)}, u32[]{:S(2)}, u32[]{:S(2)}) collective-permute-start(f32[1,1,2048]{2,1,0:T(1,128)S(1)} %get-tuple-element.148), channel_id=1, source_target_pairs={{0,1},{1,2},{2,3},{3,4},{4,5},{5,6},{6,7},{7,8},{8,9},{9,10},{10,1... | collective-permute-start | bytes 24584 | tf_op jit(solution)/shard_map/ppermute | solution.py:19
  70.1 9.8 %collective-permute-start.12 = (f32[1,1,2048]{2,1,0:T(1,128)S(1)}, f32[1,1,2048]{2,1,0:T(1,128)S(1)}, u32[]{:S(2)}, u32[]{:S(2)}) collective-permute-start(f32[1,1,2048]{2,1,0:T(1,128)S(1)} %get-tuple-element.143), channel_id=1, source_target_pairs={{1,0},{2,1},{3,2},{4,3},{5,4},{6,5},{7,6},{8,7},{9,8},{10,9},{11,1... | collective-permute-start | bytes 24584 | tf_op jit(solution)/shard_map/ppermute | solution.py:21
  72.0 8.6 %collective-permute-start.13 = (f32[1,1,2048]{2,1,0:T(1,128)S(1)}, f32[1,1,2048]{2,1,0:T(1,128)S(1)}, u32[]{:S(2)}, u32[]{:S(2)}) collective-permute-start(f32[1,1,2048]{2,1,0:T(1,128)S(1)} %get-tuple-element.142), channel_id=1, source_target_pairs={{0,1},{1,2},{2,3},{3,4},{4,5},{5,6},{6,7},{7,8},{8,9},{9,10},{10,1... | collective-permute-start | bytes 24584 | tf_op jit(solution)/shard_map/ppermute | solution.py:19
  80.8 9.8 %collective-permute-start.14 = (f32[1,1,2048]{2,1,0:T(1,128)S(1)}, f32[1,1,2048]{2,1,0:T(1,128)S(1)}, u32[]{:S(2)}, u32[]{:S(2)}) collective-permute-start(f32[1,1,2048]{2,1,0:T(1,128)S(1)} %get-tuple-element.137), channel_id=1, source_target_pairs={{1,0},{2,1},{3,2},{4,3},{5,4},{6,5},{7,6},{8,7},{9,8},{10,9},{11,1... | collective-permute-start | bytes 24584 | tf_op jit(solution)/shard_map/ppermute | solution.py:21
  82.8 8.6 %collective-permute-start.15 = (f32[1,1,2048]{2,1,0:T(1,128)S(1)}, f32[1,1,2048]{2,1,0:T(1,128)S(1)}, u32[]{:S(2)}, u32[]{:S(2)}) collective-permute-start(f32[1,1,2048]{2,1,0:T(1,128)S(1)} %get-tuple-element.136), channel_id=1, source_target_pairs={{0,1},{1,2},{2,3},{3,4},{4,5},{5,6},{6,7},{7,8},{8,9},{9,10},{10,1... | collective-permute-start | bytes 24584 | tf_op jit(solution)/shard_map/ppermute | solution.py:19
  91.5 15.4 %collective-permute-start.16 = (f32[1,16,2048]{2,1,0:T(8,128)S(1)}, f32[1,16,2048]{2,1,0:T(8,128)S(1)}, u32[]{:S(2)}, u32[]{:S(2)}) collective-permute-start(f32[1,16,2048]{2,1,0:T(8,128)S(1)} %fusion.15), channel_id=1, source_target_pairs={{0,16},{16,32},{32,48},{48,64},{64,80},{80,96},{96,112},{112,128},... | collective-permute-start | bytes 393224 | tf_op jit(solution)/shard_map/ppermute | solution.py:31
  106.9 9.0 %collective-permute-start.17 = (f32[1,1,2048]{2,1,0:T(1,128)S(1)}, f32[1,1,2048]{2,1,0:T(1,128)S(1)}, u32[]{:S(2)}, u32[]{:S(2)}) collective-permute-start(f32[1,1,2048]{2,1,0:T(1,128)S(1)} %get-tuple-element.131), channel_id=1, source_target_pairs={{1,0},{2,1},{3,2},{4,3},{5,4},{6,5},{7,6},{8,7},{9,8},{10,9},{11,1... | collective-permute-start | bytes 24584 | tf_op jit(solution)/shard_map/ppermute | solution.py:21
  108.8 7.7 %collective-permute-start.18 = (f32[1,1,2048]{2,1,0:T(1,128)S(1)}, f32[1,1,2048]{2,1,0:T(1,128)S(1)}, u32[]{:S(2)}, u32[]{:S(2)}) collective-permute-start(f32[1,1,2048]{2,1,0:T(1,128)S(1)} %get-tuple-element.130), channel_id=1, source_target_pairs={{0,1},{1,2},{2,3},{3,4},{4,5},{5,6},{6,7},{7,8},{8,9},{9,10},{10,1... | collective-permute-start | bytes 24584 | tf_op jit(solution)/shard_map/ppermute | solution.py:19
  116.8 11.3 %collective-permute-start.19 = (f32[1,1,2048]{2,1,0:T(1,128)S(1)}, f32[1,1,2048]{2,1,0:T(1,128)S(1)}, u32[]{:S(2)}, u32[]{:S(2)}) collective-permute-start(f32[1,1,2048]{2,1,0:T(1,128)S(1)} %get-tuple-element.125), channel_id=1, source_target_pairs={{1,0},{2,1},{3,2},{4,3},{5,4},{6,5},{7,6},{8,7},{9,8},{10,9},{11,1... | collective-permute-start | bytes 24584 | tf_op jit(solution)/shard_map/ppermute | solution.py:21
  118.7 10.1 %collective-permute-start.20 = (f32[1,1,2048]{2,1,0:T(1,128)S(1)}, f32[1,1,2048]{2,1,0:T(1,128)S(1)}, u32[]{:S(2)}, u32[]{:S(2)}) collective-permute-start(f32[1,1,2048]{2,1,0:T(1,128)S(1)} %get-tuple-element.124), channel_id=1, source_target_pairs={{0,1},{1,2},{2,3},{3,4},{4,5},{5,6},{6,7},{7,8},{8,9},{9,10},{10,1... | collective-permute-start | bytes 24584 | tf_op jit(solution)/shard_map/ppermute | solution.py:19
  129.0 9.8 %collective-permute-start.21 = (f32[1,1,2048]{2,1,0:T(1,128)S(1)}, f32[1,1,2048]{2,1,0:T(1,128)S(1)}, u32[]{:S(2)}, u32[]{:S(2)}) collective-permute-start(f32[1,1,2048]{2,1,0:T(1,128)S(1)} %get-tuple-element.119), channel_id=1, source_target_pairs={{1,0},{2,1},{3,2},{4,3},{5,4},{6,5},{7,6},{8,7},{9,8},{10,9},{11,1... | collective-permute-start | bytes 24584 | tf_op jit(solution)/shard_map/ppermute | solution.py:21
  130.9 8.6 %collective-permute-start.22 = (f32[1,1,2048]{2,1,0:T(1,128)S(1)}, f32[1,1,2048]{2,1,0:T(1,128)S(1)}, u32[]{:S(2)}, u32[]{:S(2)}) collective-permute-start(f32[1,1,2048]{2,1,0:T(1,128)S(1)} %get-tuple-element.118), channel_id=1, source_target_pairs={{0,1},{1,2},{2,3},{3,4},{4,5},{5,6},{6,7},{7,8},{8,9},{9,10},{10,1... | collective-permute-start | bytes 24584 | tf_op jit(solution)/shard_map/ppermute | solution.py:19
  139.8 9.8 %collective-permute-start.23 = (f32[1,1,2048]{2,1,0:T(1,128)S(1)}, f32[1,1,2048]{2,1,0:T(1,128)S(1)}, u32[]{:S(2)}, u32[]{:S(2)}) collective-permute-start(f32[1,1,2048]{2,1,0:T(1,128)S(1)} %get-tuple-element.113), channel_id=1, source_target_pairs={{1,0},{2,1},{3,2},{4,3},{5,4},{6,5},{7,6},{8,7},{9,8},{10,9},{11,1... | collective-permute-start | bytes 24584 | tf_op jit(solution)/shard_map/ppermute | solution.py:21
  141.7 8.6 %collective-permute-start.24 = (f32[1,1,2048]{2,1,0:T(1,128)S(1)}, f32[1,1,2048]{2,1,0:T(1,128)S(1)}, u32[]{:S(2)}, u32[]{:S(2)}) collective-permute-start(f32[1,1,2048]{2,1,0:T(1,128)S(1)} %get-tuple-element.112), channel_id=1, source_target_pairs={{0,1},{1,2},{2,3},{3,4},{4,5},{5,6},{6,7},{7,8},{8,9},{9,10},{10,1... | collective-permute-start | bytes 24584 | tf_op jit(solution)/shard_map/ppermute | solution.py:19
  150.6 9.8 %collective-permute-start.25 = (f32[1,1,2048]{2,1,0:T(1,128)S(1)}, f32[1,1,2048]{2,1,0:T(1,128)S(1)}, u32[]{:S(2)}, u32[]{:S(2)}) collective-permute-start(f32[1,1,2048]{2,1,0:T(1,128)S(1)} %get-tuple-element.107), channel_id=1, source_target_pairs={{1,0},{2,1},{3,2},{4,3},{5,4},{6,5},{7,6},{8,7},{9,8},{10,9},{11,1... | collective-permute-start | bytes 24584 | tf_op jit(solution)/shard_map/ppermute | solution.py:21
  152.5 8.6 %collective-permute-start.26 = (f32[1,1,2048]{2,1,0:T(1,128)S(1)}, f32[1,1,2048]{2,1,0:T(1,128)S(1)}, u32[]{:S(2)}, u32[]{:S(2)}) collective-permute-start(f32[1,1,2048]{2,1,0:T(1,128)S(1)} %get-tuple-element.106), channel_id=1, source_target_pairs={{0,1},{1,2},{2,3},{3,4},{4,5},{5,6},{6,7},{7,8},{8,9},{9,10},{10,1... | collective-permute-start | bytes 24584 | tf_op jit(solution)/shard_map/ppermute | solution.py:19
  161.3 9.8 %collective-permute-start.27 = (f32[1,1,2048]{2,1,0:T(1,128)S(1)}, f32[1,1,2048]{2,1,0:T(1,128)S(1)}, u32[]{:S(2)}, u32[]{:S(2)}) collective-permute-start(f32[1,1,2048]{2,1,0:T(1,128)S(1)} %get-tuple-element.101), channel_id=1, source_target_pairs={{1,0},{2,1},{3,2},{4,3},{5,4},{6,5},{7,6},{8,7},{9,8},{10,9},{11,1... | collective-permute-start | bytes 24584 | tf_op jit(solution)/shard_map/ppermute | solution.py:21
  163.3 8.6 %collective-permute-start.28 = (f32[1,1,2048]{2,1,0:T(1,128)S(1)}, f32[1,1,2048]{2,1,0:T(1,128)S(1)}, u32[]{:S(2)}, u32[]{:S(2)}) collective-permute-start(f32[1,1,2048]{2,1,0:T(1,128)S(1)} %get-tuple-element.100), channel_id=1, source_target_pairs={{0,1},{1,2},{2,3},{3,4},{4,5},{5,6},{6,7},{7,8},{8,9},{9,10},{10,1... | collective-permute-start | bytes 24584 | tf_op jit(solution)/shard_map/ppermute | solution.py:19
  172.1 9.8 %collective-permute-start.29 = (f32[1,1,2048]{2,1,0:T(1,128)S(1)}, f32[1,1,2048]{2,1,0:T(1,128)S(1)}, u32[]{:S(2)}, u32[]{:S(2)}) collective-permute-start(f32[1,1,2048]{2,1,0:T(1,128)S(1)} %get-tuple-element.95), channel_id=1, source_target_pairs={{1,0},{2,1},{3,2},{4,3},{5,4},{6,5},{7,6},{8,7},{9,8},{10,9},{11,1... | collective-permute-start | bytes 24584 | tf_op jit(solution)/shard_map/ppermute | solution.py:21
  174.0 8.6 %collective-permute-start.30 = (f32[1,1,2048]{2,1,0:T(1,128)S(1)}, f32[1,1,2048]{2,1,0:T(1,128)S(1)}, u32[]{:S(2)}, u32[]{:S(2)}) collective-permute-start(f32[1,1,2048]{2,1,0:T(1,128)S(1)} %get-tuple-element.94), channel_id=1, source_target_pairs={{0,1},{1,2},{2,3},{3,4},{4,5},{5,6},{6,7},{7,8},{8,9},{9,10},{10,1... | collective-permute-start | bytes 24584 | tf_op jit(solution)/shard_map/ppermute | solution.py:19
  182.9 9.8 %collective-permute-start.31 = (f32[1,1,2048]{2,1,0:T(1,128)S(1)}, f32[1,1,2048]{2,1,0:T(1,128)S(1)}, u32[]{:S(2)}, u32[]{:S(2)}) collective-permute-start(f32[1,1,2048]{2,1,0:T(1,128)S(1)} %get-tuple-element.89), channel_id=1, source_target_pairs={{1,0},{2,1},{3,2},{4,3},{5,4},{6,5},{7,6},{8,7},{9,8},{10,9},{11,1... | collective-permute-start | bytes 24584 | tf_op jit(solution)/shard_map/ppermute | solution.py:21
  184.8 8.6 %collective-permute-start.32 = (f32[1,1,2048]{2,1,0:T(1,128)S(1)}, f32[1,1,2048]{2,1,0:T(1,128)S(1)}, u32[]{:S(2)}, u32[]{:S(2)}) collective-permute-start(f32[1,1,2048]{2,1,0:T(1,128)S(1)} %get-tuple-element.88), channel_id=1, source_target_pairs={{0,1},{1,2},{2,3},{3,4},{4,5},{5,6},{6,7},{7,8},{8,9},{9,10},{10,1... | collective-permute-start | bytes 24584 | tf_op jit(solution)/shard_map/ppermute | solution.py:19
  193.5 9.0 %collective-permute-start.33 = (f32[1,16,2048]{2,1,0:T(8,128)S(1)}, f32[1,16,2048]{2,1,0:T(8,128)S(1)}, u32[]{:S(2)}, u32[]{:S(2)}) collective-permute-start(f32[1,16,2048]{2,1,0:T(8,128)S(1)} %fusion.31), channel_id=1, source_target_pairs={{0,16},{16,32},{32,48},{48,64},{64,80},{80,96},{96,112},{112,128},... | collective-permute-start | bytes 393224 | tf_op jit(solution)/shard_map/ppermute | solution.py:31
  (6 other events, 162.8 us)
Sparse Core Ops, SparseCore 0:
  203.3 140.6 all-gather.1
where the time goes:
time: 440 us; the launch traced here: 437 us
  waiting for transfers between devices  171 us (39%)
  starting transfers between devices  153 us (35%)
  other arithmetic  92 us (21%)
  between operations  14.7 us (3%)
  local copies, waits for them, and re-layouts  5.51 us (1%)
    all_gather x1, waiting for transfers between devices, shards(): residuals = lax.all_gather(coarse_residual, 'tm', axis=0, tiled=True)  141 us
    ppermute x16, starting transfers between devices, with_halo(): lax.ppermute(tail, axis, [(i, (i + 1) % count) for i in range(count)])  116 us
    dynamic_update_slice x32, other arithmetic, shards(): unused_last, sequence = lax.scan(accumulate, last_error, residuals)  52.8 us
    ppermute x16, starting transfers between devices, with_halo(): lax.ppermute(head, axis, [((i + 1) % count, i) for i in range(count)])  31.5 us
    add x32, other arithmetic, accumulate(): following = factor * carry + term  31.5 us
    ppermute x2, waiting for transfers between devices, passed_along(): return lax.ppermute(value, axis, pairs)  18.6 us
    ppermute x16, waiting for transfers between devices, with_halo(): lax.ppermute(tail, axis, [(i, (i + 1) % count) for i in range(count)])  11.8 us
  transfers between devices with their start and end apart: 35, of which 19 were waited for; matrix products, arithmetic and copies ran while one was open for 1% of the time, Pallas kernels for 0%

commit v1 on v0

v1 whole, which is shorter than its diff:
```python
import jax
import jax.numpy as jnp
from jax import lax
from jax.experimental import pallas as pl
from jax.experimental.pallas import tpu as pltpu
from jax.sharding import PartitionSpec as P

M = 8
nonlinear_weight = 0.05


def load_interleaved(dst, source, first, blocks):
    for c in range(source.shape[0]):
        for i in range(blocks):
            dst[c, i] = source[c, pl.ds(first + i, 8, stride=blocks), :]


def steps(state, other, coefs, blocks):
    tiles = state.shape[0]
    lane = lax.broadcasted_iota(jnp.int32, (8, 128), 1)
    is_last, is_first = lane == 127, lane == 0

    def one(src, dst):
        for i in range(blocks):
            to_left = lambda c: pltpu.roll(src[c % tiles, i], 127, 1)
            to_right = lambda c: pltpu.roll(src[c % tiles, i], 1, 1)
            ahead, behind, here = to_left(0), to_right(-1), to_right(0)
            for c in range(tiles):
                u = src[c, i]
                above = src[c, i + 1] if i + 1 < blocks else pltpu.roll(src[c, 0], 7, 0)
                below = src[c, i - 1] if i > 0 else pltpu.roll(src[c, blocks - 1], 1, 0)
                following = to_left(c + 1)
                right = jnp.where(is_last, following, ahead)
                left = jnp.where(is_first, behind, here)
                ahead, behind, here = following, here, to_right(c + 1)
                spread = coefs[2, c, i] * ((above + below) + (right + left))
                along = (coefs[0, c, i] + (0.5 * nonlinear_weight) * u) * (right - left)
                across = coefs[1, c, i] * (above - below)
                dst[c, i] = ((coefs[3, c, i] * u + spread) - along) - across

    def pair(_, carry):
        one(state, other)
        one(other, state)
        return carry

    lax.fori_loop(0, M // 2, pair, 0)


def propagate_kernel(
    cells, drift, diffusivity, rate, before, after, second_out, first_out, term_out, rows, coef_rows, state, other, coefs
):
    height, width = cells.shape
    tiles = width // 128
    for c in range(tiles):
        cols = slice(c * 128, c * 128 + 128)
        rows[c, 0:height] = before[0:height, cols]
        rows[c, height : 2 * height] = cells[:, cols]
        rows[c, 2 * height :] = after[0:height, cols]
        for k in range(3):
            scale = 0.5 if k < 2 else 1.0
            own = drift[k, :, cols] if k < 2 else diffusivity[:, cols]
            part = slice((k + 1) * height, (k + 2) * height)
            coef_rows[k, c, 0:height] = scale * before[part, cols]
            coef_rows[k, c, height : 2 * height] = scale * own
            coef_rows[k, c, 2 * height :] = scale * after[part, cols]

    def phase(first, blocks, out):
        load_interleaved(state, rows, first, blocks)
        for k in range(3):
            load_interleaved(coefs.at[k], coef_rows.at[k], first, blocks)
        for c in range(tiles):
            for i in range(blocks):
                coefs[3, c, i] = 1.0 - 4.0 * coefs[2, c, i]
        steps(state, other, coefs, blocks)
        for c in range(tiles):
            for i in range(blocks):
                rows[c, pl.ds(first + i, 8, stride=blocks), :] = state[c, i]
        for c in range(tiles):
            out[:, c * 128 : c * 128 + 128] = rows[c, height : 2 * height]

    phase(0, 6, first_out)
    phase(8, 4, second_out)
    for r in range(height // 8):
        for c in range(tiles):
            part = (slice(r * 8, r * 8 + 8), slice(c * 128, c * 128 + 128))
            term_out[r * tiles + c] = second_out[part] - jnp.exp(-rate[part]) * first_out[part]


def propagate(cells, drift, diffusivity, rate, before, after):
    height, width = cells.shape
    tiles = height // 8 * (width // 128)
    shape = lambda *s: jax.ShapeDtypeStruct(s, jnp.float32)
    return pl.pallas_call(
        propagate_kernel,
        out_shape=(shape(height, width), shape(height, width), shape(tiles, 8, 128)),
        scratch_shapes=[
            pltpu.VMEM((width // 128, 3 * height, 128), jnp.float32),
            pltpu.VMEM((3, width // 128, 3 * height, 128), jnp.float32),
            pltpu.VMEM((width // 128, 6, 8, 128), jnp.float32),
            pltpu.VMEM((width // 128, 6, 8, 128), jnp.float32),
            pltpu.VMEM((4, width // 128, 6, 8, 128), jnp.float32),
        ],
        compiler_params=pltpu.CompilerParams(vmem_limit_bytes=32 * 1024 * 1024),
        name="propagate",
    )(cells, drift, diffusivity, rate, before, after)


def solve_kernel(terms, rate, points):
    intervals = terms.shape[0]
    decay = jnp.exp(-rate[...])
    power = decay
    for _ in range(intervals.bit_length() - 1):
        power = power * power
    closing = terms[0]
    for j in range(1, intervals):
        closing = decay * closing + terms[j]
    value = closing / (1.0 - power)
    for j in range(intervals):
        value = decay * value + terms[j]
        points[(j + 2) % intervals] = value


def coarse_solve(terms, rate):
    return pl.pallas_call(
        solve_kernel,
        out_shape=jax.ShapeDtypeStruct(terms.shape, jnp.float32),
        name="coarse_solve",
    )(terms, rate)


def passed_along(value, axis, steps):
    count = lax.axis_size(axis)
    return lax.ppermute(value, axis, [(i, (i + steps) % count) for i in range(count)])


def to_tiles(value):
    height, width = value.shape
    return value.reshape(height // 8, 8, width // 128, 128).transpose(0, 2, 1, 3).reshape(-1, 8, 128)


def from_tiles(value, height, width):
    return value.reshape(height // 8, width // 128, 8, 128).transpose(0, 2, 1, 3).reshape(height, width)


def shards(cstates, drift, diffusivity, coarse_rate):
    cells = cstates[0]
    height, width = cells.shape
    message = jnp.concatenate([cells, drift[0], drift[1], diffusivity], axis=0)
    before = passed_along(message, "space", 1)
    after = passed_along(message, "space", -1)
    second, first, term = propagate(cells, drift, diffusivity, coarse_rate, before, after)
    rate = lax.dynamic_index_in_dim(to_tiles(coarse_rate), lax.axis_index("tm"), 0, keepdims=False)
    second_two_on = passed_along(second, "tm", 2)
    first_one_on = passed_along(first, "tm", 1)
    terms = lax.all_to_all(term, "tm", 0, 0, tiled=True)
    points = coarse_solve(terms, rate)
    points = lax.all_to_all(points, "tm", 0, 0, tiled=True)
    cpoints = from_tiles(points, height, width)
    residual = second_two_on - first_one_on
    return cpoints[None], residual[None]


def solution(mesh):
    placed = (P("tm", "space", None), P(None, "space", None), P("space", None), P("space", None))
    return jax.shard_map(
        shards,
        mesh=mesh,
        in_specs=placed,
        out_specs=(P("tm", "space", None), P("tm", "space", None)),
        check_vma=False,
    )
```

time: 440 us -> 78.7 us (0.18)
  the two profiles are of different devices: /device:TPU:6 before, /device:TPU:7 now
where the time goes in v1:
time: 78.7 us; the launch traced here: 78.3 us
  waiting for transfers between devices  34 us (43%)
  starting transfers between devices  33.7 us (43%)
  Pallas kernels  6.22 us (8%)
  local copies, waits for them, and re-layouts  2.98 us (4%)
    all_to_all x1, starting transfers between devices, shards(): terms = lax.all_to_all(term, 'tm', 0, 0, tiled=True)  15.3 us
    ppermute x4, starting transfers between devices, passed_along(): lax.ppermute(value, axis, [(i, (i + steps) % count) for i in range(count)])  14.5 us
    all_to_all x1, waiting for transfers between devices, shards(): points = lax.all_to_all(points, 'tm', 0, 0, tiled=True)  13.8 us
    ppermute x4, waiting for transfers between devices, passed_along(): lax.ppermute(value, axis, [(i, (i + steps) % count) for i in range(count)])  12.2 us
    all_to_all x1, waiting for transfers between devices, shards(): terms = lax.all_to_all(term, 'tm', 0, 0, tiled=True)  8.02 us
    pallas_call x1, Pallas kernels, propagate(): pl.pallas_call(propagate_kernel, out_shape=(shape(height, width), shape(h...  4.52 us
    all_to_all x1, starting transfers between devices, shards(): points = lax.all_to_all(points, 'tm', 0, 0, tiled=True)  3.86 us
    pallas_call x1, Pallas kernels, coarse_solve(): pl.pallas_call(solve_kernel, out_shape=jax.ShapeDtypeStruct(terms.shape,...  1.7 us
  transfers between devices with their start and end apart: 6, of which 4 were waited for; matrix products, arithmetic and copies ran while one was open for 2% of the time, Pallas kernels for 2%

profile of v1, /device:TPU:7, one launch (start us, length us, event | category | flops | bytes accessed | tf_op | source)
XLA Modules:
  0.0 78.3 jit_solution(17749773872833319583)
XLA Ops:
  0.6 0.0 copy-start.1
  0.6 0.0 copy-start.2
  0.6 1.0 %slice_bitcast_fusion.1 = (f32[16,2048]{1,0:T(8,128)S(1)}, f32[16,2048]{1,0:T(8,128)S(1)}) fusion(f32[2,16,2048]{2,1,0:T(8,128)} %drift.1), kind=kLoop, calls=%fused_computation.3 | loop fusion | bytes 524288 | tf_op jit(solution)/shard_map/squeeze | solution.py:148
  1.7 0.0 copy-done.1
  1.7 0.0 copy-done.2
  1.7 0.0 copy-start
  1.7 0.0 copy-start.3
  1.8 5.4 %collective-permute-start = (f32[64,2048]{1,0:T(8,128)S(1)}, f32[64,2048]{1,0:T(8,128)S(1)}, u32[]{:S(2)}, u32[]{:S(2)}) collective-permute-start(f32[64,2048]{1,0:T(8,128)S(1)} %pad_maximum_fusion), channel_id=1, source_target_pairs={{0,1},{1,2},{2,3},{3,4},{4,5},{5,6},{6,7},{7,8},{8,9},{9,10},{10,1... | collective-permute-start | bytes 1572872 | tf_op jit(solution)/shard_map/ppermute | solution.py:133
  7.2 1.9 %collective-permute-start.1 = (f32[64,2048]{1,0:T(8,128)S(1)}, f32[64,2048]{1,0:T(8,128)S(1)}, u32[]{:S(2)}, u32[]{:S(2)}) collective-permute-start(f32[64,2048]{1,0:T(8,128)S(1)} %pad_maximum_fusion), channel_id=1, source_target_pairs={{0,15},{1,0},{2,1},{3,2},{4,3},{5,4},{6,5},{7,6},{8,7},{9,8},{10,9... | collective-permute-start | bytes 1572872 | tf_op jit(solution)/shard_map/ppermute | solution.py:133
  9.1 4.2 %collective-permute-done.before = f32[64,2048]{1,0:T(8,128)S(1)} collective-permute-done((f32[64,2048]{1,0:T(8,128)S(1)}, f32[64,2048]{1,0:T(8,128)S(1)}, u32[]{:S(2)}, u32[]{:S(2)}) %collective-permute-start) | collective-permute-done | bytes 524320 | tf_op jit(solution)/shard_map/ppermute | solution.py:133
  13.3 8.0 %collective-permute-done.1.after = f32[64,2048]{1,0:T(8,128)S(1)} collective-permute-done((f32[64,2048]{1,0:T(8,128)S(1)}, f32[64,2048]{1,0:T(8,128)S(1)}, u32[]{:S(2)}, u32[]{:S(2)}) %collective-permute-start.1) | collective-permute-done | bytes 524320 | tf_op jit(solution)/shard_map/ppermute | solution.py:133
  21.3 0.0 copy-done
  21.3 0.0 copy-done.3
  21.3 4.5 %propagate.1 = (f32[16,2048]{1,0:T(8,128)S(1)}, f32[16,2048]{1,0:T(8,128)S(1)}, f32[32,8,128]{2,1,0:T(8,128)}) custom-call(f32[16,2048]{1,0:T(8,128)S(1)} %bitcast.20, f32[2,16,2048]{2,1,0:T(8,128)S(1)} %copy-done, f32[16,2048]{1,0:T(8,128)S(1)} %copy-done.2, f32[16,2048]{1,0:T(8,128)S(1)} %copy-done.3, f32[64,2048]{1,0:T(8,128)S(1)} %collective-permute-done.before, ...), custom_call_target="tpu_custom_call" | custom-call | tf_op jit(solution)/shard_map/propagate/pallas_call | solution.py:93
  25.8 15.3 %all-to-all-start = ((f32[32,8,128]{2,1,0:T(8,128)}), f32[32,8,128]{2,1,0:T(8,128)S(1)}, u32[]{:S(2)}, u32[]{:S(2)}) async-start(f32[32,8,128]{2,1,0:T(8,128)} %get-tuple-element.5), calls=%async_computation | async-start | bytes 262144 | tf_op jit(solution)/shard_map/all_to_all | solution.py:155
  41.2 4.0 %collective-permute-start.2 = (f32[16,2048]{1,0:T(8,128)S(1)}, f32[16,2048]{1,0:T(8,128)S(1)}, u32[]{:S(2)}, u32[]{:S(2)}) collective-permute-start(f32[16,2048]{1,0:T(8,128)S(1)} %get-tuple-element.6), channel_id=1, source_target_pairs={{0,32},{16,48},{32,64},{48,80},{64,96},{80,112},{96,128},{112,144}... | collective-permute-start | bytes 393224 | tf_op jit(solution)/shard_map/ppermute | solution.py:133
  45.2 3.1 %collective-permute-start.3 = (f32[16,2048]{1,0:T(8,128)S(1)}, f32[16,2048]{1,0:T(8,128)S(1)}, u32[]{:S(2)}, u32[]{:S(2)}) collective-permute-start(f32[16,2048]{1,0:T(8,128)S(1)} %get-tuple-element.7), channel_id=1, source_target_pairs={{0,16},{16,32},{32,48},{48,64},{64,80},{80,96},{96,112},{112,128},... | collective-permute-start | bytes 393224 | tf_op jit(solution)/shard_map/ppermute | solution.py:133
  48.3 0.6 dynamic-slice_bitcast_fusion.rate
  48.9 8.0 %all-to-all-done.terms = f32[32,8,128]{2,1,0:T(8,128)S(1)} async-done(((f32[32,8,128]{2,1,0:T(8,128)}), f32[32,8,128]{2,1,0:T(8,128)S(1)}, u32[]{:S(2)}, u32[]{:S(2)}) %all-to-all-start) | async-done | bytes 131104 | tf_op jit(solution)/shard_map/all_to_all | solution.py:155
  56.9 0.0 copy-start.4
  56.9 0.7 copy-done.4
  57.6 1.7 %coarse_solve.1 = f32[32,8,128]{2,1,0:T(8,128)} custom-call(f32[32,8,128]{2,1,0:T(8,128)} %copy-done.4, f32[8,128]{1,0:T(8,128)} %dynamic-slice_bitcast_fusion.rate), custom_call_target="tpu_custom_call" | custom-call | tf_op jit(solution)/shard_map/coarse_solve/pallas_call | solution.py:124
  59.3 3.9 %all-to-all-start.1 = ((f32[32,8,128]{2,1,0:T(8,128)}), f32[32,8,128]{2,1,0:T(8,128)S(1)}, u32[]{:S(2)}, u32[]{:S(2)}) async-start(f32[32,8,128]{2,1,0:T(8,128)} %coarse_solve.1), calls=%async_computation.1 | async-start | bytes 262144 | tf_op jit(solution)/shard_map/all_to_all | solution.py:157
  63.2 0.0 collective-permute-done.2
  63.2 0.0 collective-permute-done.3
  63.2 0.7 subtract_bitcast_fusion
  63.9 13.8 %all-to-all-done.1 = f32[32,8,128]{2,1,0:T(8,128)S(1)} async-done(((f32[32,8,128]{2,1,0:T(8,128)}), f32[32,8,128]{2,1,0:T(8,128)S(1)}, u32[]{:S(2)}, u32[]{:S(2)}) %all-to-all-start.1) | async-done | bytes 131104 | tf_op jit(solution)/shard_map/all_to_all | solution.py:157
  77.7 0.7 copy.7
  (1 shorter events, 0.0 us)
Async XLA Ops:
  0.6 1.1 %copy-start.1 = (f32[1,16,2048]{2,1,0:T(8,128)S(1)}, f32[1,16,2048]{2,1,0:T(8,128)}, u32[]{:S(2)}) copy-start(f32[1,16,2048]{2,1,0:T(8,128)} %param.4) | copy-start | bytes 393220
  0.6 1.1 %copy-start.2 = (f32[16,2048]{1,0:T(8,128)S(1)}, f32[16,2048]{1,0:T(8,128)}, u32[]{:S(2)}) copy-start(f32[16,2048]{1,0:T(8,128)} %diffusivity.1) | copy-start | bytes 393220
  1.7 19.6 %copy-start = (f32[2,16,2048]{2,1,0:T(8,128)S(1)}, f32[2,16,2048]{2,1,0:T(8,128)}, u32[]{:S(2)}) copy-start(f32[2,16,2048]{2,1,0:T(8,128)} %drift.1) | copy-start | bytes 786436
  1.7 19.6 %copy-start.3 = (f32[16,2048]{1,0:T(8,128)S(1)}, f32[16,2048]{1,0:T(8,128)}, u32[]{:S(2)}) copy-start(f32[16,2048]{1,0:T(8,128)} %rate.1) | copy-start | bytes 393220
  1.8 11.5 %collective-permute-start = (f32[64,2048]{1,0:T(8,128)S(1)}, f32[64,2048]{1,0:T(8,128)S(1)}, u32[]{:S(2)}, u32[]{:S(2)}) collective-permute-start(f32[64,2048]{1,0:T(8,128)S(1)} %pad_maximum_fusion), channel_id=1, source_target_pairs={{0,1},{1,2},{2,3},{3,4},{4,5},{5,6},{6,7},{7,8},{8,9},{9,10},{10,1... | collective-permute-start | bytes 1572872 | tf_op jit(solution)/shard_map/ppermute | solution.py:133
  7.2 14.1 %collective-permute-start.1 = (f32[64,2048]{1,0:T(8,128)S(1)}, f32[64,2048]{1,0:T(8,128)S(1)}, u32[]{:S(2)}, u32[]{:S(2)}) collective-permute-start(f32[64,2048]{1,0:T(8,128)S(1)} %pad_maximum_fusion), channel_id=1, source_target_pairs={{0,15},{1,0},{2,1},{3,2},{4,3},{5,4},{6,5},{7,6},{8,7},{9,8},{10,9... | collective-permute-start | bytes 1572872 | tf_op jit(solution)/shard_map/ppermute | solution.py:133
  25.8 31.1 %all-to-all-start = ((f32[32,8,128]{2,1,0:T(8,128)}), f32[32,8,128]{2,1,0:T(8,128)S(1)}, u32[]{:S(2)}, u32[]{:S(2)}) async-start(f32[32,8,128]{2,1,0:T(8,128)} %get-tuple-element.5), calls=%async_computation | async-start | bytes 262144 | tf_op jit(solution)/shard_map/all_to_all | solution.py:155
  41.2 22.0 %collective-permute-start.2 = (f32[16,2048]{1,0:T(8,128)S(1)}, f32[16,2048]{1,0:T(8,128)S(1)}, u32[]{:S(2)}, u32[]{:S(2)}) collective-permute-start(f32[16,2048]{1,0:T(8,128)S(1)} %get-tuple-element.6), channel_id=1, source_target_pairs={{0,32},{16,48},{32,64},{48,80},{64,96},{80,112},{96,128},{112,144}... | collective-permute-start | bytes 393224 | tf_op jit(solution)/shard_map/ppermute | solution.py:133
  45.2 18.0 %collective-permute-start.3 = (f32[16,2048]{1,0:T(8,128)S(1)}, f32[16,2048]{1,0:T(8,128)S(1)}, u32[]{:S(2)}, u32[]{:S(2)}) collective-permute-start(f32[16,2048]{1,0:T(8,128)S(1)} %get-tuple-element.7), channel_id=1, source_target_pairs={{0,16},{16,32},{32,48},{48,64},{64,80},{80,96},{96,112},{112,128},... | collective-permute-start | bytes 393224 | tf_op jit(solution)/shard_map/ppermute | solution.py:133
  56.9 0.7 copy-start.4
  59.3 18.4 %all-to-all-start.1 = ((f32[32,8,128]{2,1,0:T(8,128)}), f32[32,8,128]{2,1,0:T(8,128)S(1)}, u32[]{:S(2)}, u32[]{:S(2)}) async-start(f32[32,8,128]{2,1,0:T(8,128)} %coarse_solve.1), calls=%async_computation.1 | async-start | bytes 262144 | tf_op jit(solution)/shard_map/all_to_all | solution.py:157

commit v2 on v1

--- a/solution.py
+++ b/solution.py
@@ -47,22 +47,31 @@
 
 
 def propagate_kernel(
-    cells, drift, diffusivity, rate, before, after, second_out, first_out, term_out, rows, coef_rows, state, other, coefs
+    parity, cells, drift, diffusivity, rate, inner, outer, second_out, first_out, term_out, rows, coef_rows, state, other, coefs
 ):
     height, width = cells.shape
     tiles = width // 128
-    for c in range(tiles):
-        cols = slice(c * 128, c * 128 + 128)
-        rows[c, 0:height] = before[0:height, cols]
-        rows[c, height : 2 * height] = cells[:, cols]
-        rows[c, 2 * height :] = after[0:height, cols]
-        for k in range(3):
-            scale = 0.5 if k < 2 else 1.0
-            own = drift[k, :, cols] if k < 2 else diffusivity[:, cols]
-            part = slice((k + 1) * height, (k + 2) * height)
-            coef_rows[k, c, 0:height] = scale * before[part, cols]
-            coef_rows[k, c, height : 2 * height] = scale * own
-            coef_rows[k, c, 2 * height :] = scale * after[part, cols]
+    def gather(before, after):
+        for c in range(tiles):
+            cols = slice(c * 128, c * 128 + 128)
+            rows[c, 0:height] = before[0:height, cols]
+            rows[c, height : 2 * height] = cells[:, cols]
+            rows[c, 2 * height :] = after[0:height, cols]
+            for k in range(3):
+                scale = 0.5 if k < 2 else 1.0
+                own = drift[k, :, cols] if k < 2 else diffusivity[:, cols]
+                part = slice((k + 1) * height, (k + 2) * height)
+                coef_rows[k, c, 0:height] = scale * before[part, cols]
+                coef_rows[k, c, height : 2 * height] = scale * own
+                coef_rows[k, c, 2 * height :] = scale * after[part, cols]
+
+    @pl.when(parity[0] == 0)
+    def _():
+        gather(outer, inner)
+
+    @pl.when(parity[0] == 1)
+    def _():
+        gather(inner, outer)
 
     def phase(first, blocks, out):
         load_interleaved(state, rows, first, blocks)
@@ -86,7 +95,7 @@
             term_out[r * tiles + c] = second_out[part] - jnp.exp(-rate[part]) * first_out[part]
 
 
-def propagate(cells, drift, diffusivity, rate, before, after):
+def propagate(parity, cells, drift, diffusivity, rate, inner, outer):
     height, width = cells.shape
     tiles = height // 8 * (width // 128)
     shape = lambda *s: jax.ShapeDtypeStruct(s, jnp.float32)
@@ -100,30 +109,39 @@
             pltpu.VMEM((width // 128, 6, 8, 128), jnp.float32),
             pltpu.VMEM((4, width // 128, 6, 8, 128), jnp.float32),
         ],
+        in_specs=[pl.BlockSpec(memory_space=pltpu.SMEM)] + [pl.BlockSpec(memory_space=pltpu.VMEM)] * 6,
         compiler_params=pltpu.CompilerParams(vmem_limit_bytes=32 * 1024 * 1024),
         name="propagate",
-    )(cells, drift, diffusivity, rate, before, after)
+    )(parity, cells, drift, diffusivity, rate, inner, outer)
 
 
 def solve_kernel(terms, rate, points):
-    intervals = terms.shape[0]
-    decay = jnp.exp(-rate[...])
-    power = decay
-    for _ in range(intervals.bit_length() - 1):
-        power = power * power
-    closing = terms[0]
-    for j in range(1, intervals):
-        closing = decay * closing + terms[j]
-    value = closing / (1.0 - power)
-    for j in range(intervals):
-        value = decay * value + terms[j]
-        points[(j + 2) % intervals] = value
+    intervals, length = terms.shape[0], 8
+    chains = intervals // length
+    powers = [jnp.exp(-rate[...])]
+    for _ in range(length - 1):
+        powers.append(powers[-1] * powers[0])
+    sums = [[terms[c * length]] for c in range(chains)]
+    for k in range(1, length):
+        for c in range(chains):
+            sums[c].append(powers[0] * sums[c][-1] + terms[c * length + k])
+    jump = powers[-1]
+    closing, whole = sums[0][-1], jump
+    for c in range(1, chains):
+        closing = jump * closing + sums[c][-1]
+        whole = whole * jump
+    carry = closing / (1.0 - whole)
+    for c in range(chains):
+        for k in range(length):
+            points[(c * length + k + 2) % intervals] = powers[k] * carry + sums[c][k]
+        carry = jump * carry + sums[c][-1]
 
 
 def coarse_solve(terms, rate):
     return pl.pallas_call(
         solve_kernel,
         out_shape=jax.ShapeDtypeStruct(terms.shape, jnp.float32),
+        compiler_params=pltpu.CompilerParams(vmem_limit_bytes=2 * 1024 * 1024),
         name="coarse_solve",
     )(terms, rate)
 
@@ -146,17 +164,18 @@
     cells = cstates[0]
     height, width = cells.shape
     message = jnp.concatenate([cells, drift[0], drift[1], diffusivity], axis=0)
-    before = passed_along(message, "space", 1)
-    after = passed_along(message, "space", -1)
-    second, first, term = propagate(cells, drift, diffusivity, coarse_rate, before, after)
+    strips = lax.axis_size("space")
+    outer = lax.ppermute(message, "space", [(i, (((i + 1) ^ 1) - 1) % strips) for i in range(strips)])
+    inner = lax.ppermute(message, "space", [(i, i ^ 1) for i in range(strips)])
+    parity = (lax.axis_index("space") % 2).reshape(1)
+    second, first, term = propagate(parity, cells, drift, diffusivity, coarse_rate, inner, outer)
     rate = lax.dynamic_index_in_dim(to_tiles(coarse_rate), lax.axis_index("tm"), 0, keepdims=False)
-    second_two_on = passed_along(second, "tm", 2)
-    first_one_on = passed_along(first, "tm", 1)
+    ahead = passed_along(second, "tm", 1) - first
+    residual = passed_along(ahead, "tm", 1)
     terms = lax.all_to_all(term, "tm", 0, 0, tiled=True)
     points = coarse_solve(terms, rate)
     points = lax.all_to_all(points, "tm", 0, 0, tiled=True)
     cpoints = from_tiles(points, height, width)
-    residual = second_two_on - first_one_on
     return cpoints[None], residual[None]
 
 

time: 78.7 us -> 80.9 us (1.028)
  waiting for transfers between devices: 34 us -> 39.7 us
  starting transfers between devices: 33.7 us -> 32.4 us
  Pallas kernels: 6.22 us -> 5.22 us
    all_to_all x1, waiting for transfers between devices: 13.8 us -> 0.01 us  [shards(): points = lax.all_to_all(points, 'tm', 0, 0, tiled=True)]
    ppermute x4 -> x2, starting transfers between devices: 14.5 us -> 4.95 us  [passed_along(): lax.ppermute(value, axis, [(i, (i + steps) % count) for i in range(count)])]
    ppermute x0 -> x2, waiting for transfers between devices: none -> 9.45 us  [the longest x1 9.45 us: shards(): lax.ppermute(message, 'space', [(i, ((i + 1 ^ 1) - 1) % strips) for i in...]
    ppermute x0 -> x2, starting transfers between devices: none -> 7.35 us  [the longest x1 4.63 us: shards(): lax.ppermute(message, 'space', [(i, ((i + 1 ^ 1) - 1) % strips) for i in...]
    all_to_all x1, waiting for transfers between devices: 8.02 us -> 14.4 us  [shards(): terms = lax.all_to_all(term, 'tm', 0, 0, tiled=True)]
    ppermute x4 -> x2, waiting for transfers between devices: 12.2 us -> 15.9 us  [passed_along(): lax.ppermute(value, axis, [(i, (i + steps) % count) for i in range(count)])]
    pallas_call x1, Pallas kernels: 1.7 us -> 0.7 us  [coarse_solve(): pl.pallas_call(solve_kernel, out_shape=jax.ShapeDtypeStruct(terms.shape,...]
    all_to_all x1, starting transfers between devices: 15.3 us -> 16.2 us  [shards(): terms = lax.all_to_all(term, 'tm', 0, 0, tiled=True)]
  transfers between devices with their start and end apart: 6 -> 6, of which waited for: 4 -> 4; matrix products, arithmetic and copies ran while one was open for 2% -> 0% of each run, Pallas kernels for 2% -> 0%
where the time goes in v2:
time: 80.9 us; the launch traced here: 80.5 us
  waiting for transfers between devices  39.7 us (49%)
  starting transfers between devices  32.4 us (40%)
  Pallas kernels  5.22 us (6%)
  local copies, waits for them, and re-layouts  2.39 us (3%)
    all_to_all x1, starting transfers between devices, shards(): terms = lax.all_to_all(term, 'tm', 0, 0, tiled=True)  16.2 us
    ppermute x2, waiting for transfers between devices, passed_along(): lax.ppermute(value, axis, [(i, (i + steps) % count) for i in range(count)])  15.9 us
    all_to_all x1, waiting for transfers between devices, shards(): terms = lax.all_to_all(term, 'tm', 0, 0, tiled=True)  14.4 us
    ppermute x1, waiting for transfers between devices, shards(): lax.ppermute(message, 'space', [(i, ((i + 1 ^ 1) - 1) % strips) for i in...  9.45 us
    ppermute x2, starting transfers between devices, passed_along(): lax.ppermute(value, axis, [(i, (i + steps) % count) for i in range(count)])  4.95 us
    ppermute x1, starting transfers between devices, shards(): lax.ppermute(message, 'space', [(i, ((i + 1 ^ 1) - 1) % strips) for i in...  4.63 us
    pallas_call x1, Pallas kernels, propagate(): pl.pallas_call(propagate_kernel, out_shape=(shape(height, width), shape(h...  4.52 us
    all_to_all x1, starting transfers between devices, shards(): points = lax.all_to_all(points, 'tm', 0, 0, tiled=True)  3.86 us
  transfers between devices with their start and end apart: 6, of which 4 were waited for; matrix products, arithmetic and copies ran while one was open for 0% of the time, Pallas kernels for 0%

profile of v2, /device:TPU:7, one launch (start us, length us, event | category | flops | bytes accessed | tf_op | source)
XLA Modules:
  0.0 80.5 jit_solution(9810495812584685119)
XLA Ops:
  0.6 0.0 copy-start.1
  0.6 0.0 copy-start.2
  0.6 1.0 %slice_bitcast_fusion.1 = (f32[16,2048]{1,0:T(8,128)S(1)}, f32[16,2048]{1,0:T(8,128)S(1)}) fusion(f32[2,16,2048]{2,1,0:T(8,128)} %drift.1), kind=kLoop, calls=%fused_computation.2 | loop fusion | bytes 524288 | tf_op jit(solution)/shard_map/squeeze | solution.py:166
  1.7 0.0 copy-done.1
  1.7 0.0 copy-done.2
  1.7 0.0 copy-start
  1.7 0.0 copy-start.3
  1.8 2.7 %collective-permute-start = (f32[64,2048]{1,0:T(8,128)S(1)}, f32[64,2048]{1,0:T(8,128)S(1)}, u32[]{:S(2)}, u32[]{:S(2)}) collective-permute-start(f32[64,2048]{1,0:T(8,128)S(1)} %pad_maximum_fusion), channel_id=1, source_target_pairs={{0,1},{1,0},{2,3},{3,2},{4,5},{5,4},{6,7},{7,6},{8,9},{9,8},{10,11... | collective-permute-start | bytes 1572872 | tf_op jit(solution)/shard_map/ppermute | solution.py:169
  4.5 4.6 %collective-permute-start.1 = (f32[64,2048]{1,0:T(8,128)S(1)}, f32[64,2048]{1,0:T(8,128)S(1)}, u32[]{:S(2)}, u32[]{:S(2)}) collective-permute-start(f32[64,2048]{1,0:T(8,128)S(1)} %pad_maximum_fusion), channel_id=1, source_target_pairs={{0,15},{1,2},{2,1},{3,4},{4,3},{5,6},{6,5},{7,8},{8,7},{9,10},{10,... | collective-permute-start | bytes 1572872 | tf_op jit(solution)/shard_map/ppermute | solution.py:168
  9.1 0.0 collective-permute-done.inner
  9.2 9.4 %collective-permute-done.1.outer = f32[64,2048]{1,0:T(8,128)S(1)} collective-permute-done((f32[64,2048]{1,0:T(8,128)S(1)}, f32[64,2048]{1,0:T(8,128)S(1)}, u32[]{:S(2)}, u32[]{:S(2)}) %collective-permute-start.1) | collective-permute-done | bytes 524320 | tf_op jit(solution)/shard_map/ppermute | solution.py:168
  18.6 0.0 copy-done
  18.6 0.0 copy-done.3
  18.6 4.5 %propagate.1 = (f32[16,2048]{1,0:T(8,128)S(1)}, f32[16,2048]{1,0:T(8,128)S(1)}, f32[32,8,128]{2,1,0:T(8,128)}) custom-call(s32[1]{0:T(128)} %bitcast.parity, f32[16,2048]{1,0:T(8,128)S(1)} %bitcast.20, f32[2,16,2048]{2,1,0:T(8,128)S(1)} %copy-done, f32[16,2048]{1,0:T(8,128)S(1)} %copy-done.2, f32[16,2048]{1,0:T(8,128)S(1)} %copy-done.3, ...), custom_call_target="tpu_custom_call" | custom-call | tf_op jit(solution)/shard_map/propagate/pallas_call | solution.py:102
  23.1 16.2 %all-to-all-start = ((f32[32,8,128]{2,1,0:T(8,128)}), f32[32,8,128]{2,1,0:T(8,128)S(1)}, u32[]{:S(2)}, u32[]{:S(2)}) async-start(f32[32,8,128]{2,1,0:T(8,128)} %get-tuple-element.5), calls=%async_computation | async-start | bytes 262144 | tf_op jit(solution)/shard_map/all_to_all | solution.py:175
  39.4 14.4 %all-to-all-done.terms = f32[32,8,128]{2,1,0:T(8,128)S(1)} async-done(((f32[32,8,128]{2,1,0:T(8,128)}), f32[32,8,128]{2,1,0:T(8,128)S(1)}, u32[]{:S(2)}, u32[]{:S(2)}) %all-to-all-start) | async-done | bytes 131104 | tf_op jit(solution)/shard_map/all_to_all | solution.py:175
  53.7 0.7 coarse_solve.1
  54.4 3.9 %all-to-all-start.1 = ((f32[32,8,128]{2,1,0:T(8,128)}), f32[32,8,128]{2,1,0:T(8,128)S(1)}, u32[]{:S(2)}, u32[]{:S(2)}) async-start(f32[32,8,128]{2,1,0:T(8,128)} %coarse_solve.1), calls=%async_computation.1 | async-start | bytes 262144 | tf_op jit(solution)/shard_map/all_to_all | solution.py:177
  58.3 3.0 %collective-permute-start.2 = (f32[16,2048]{1,0:T(8,128)S(1)}, f32[16,2048]{1,0:T(8,128)S(1)}, u32[]{:S(2)}, u32[]{:S(2)}) collective-permute-start(f32[16,2048]{1,0:T(8,128)S(1)} %get-tuple-element.6), channel_id=1, source_target_pairs={{0,16},{16,32},{32,48},{48,64},{64,80},{80,96},{96,112},{112,128},... | collective-permute-start | bytes 393224 | tf_op jit(solution)/shard_map/ppermute | solution.py:151
  61.3 8.6 %collective-permute-done.2 = f32[16,2048]{1,0:T(8,128)S(1)} collective-permute-done((f32[16,2048]{1,0:T(8,128)S(1)}, f32[16,2048]{1,0:T(8,128)S(1)}, u32[]{:S(2)}, u32[]{:S(2)}) %collective-permute-start.2) | collective-permute-done | bytes 131104 | tf_op jit(solution)/shard_map/ppermute | solution.py:151
  70.0 1.9 %collective-permute-start.3 = (f32[16,2048]{1,0:T(8,128)S(1)}, f32[16,2048]{1,0:T(8,128)S(1)}, u32[]{:S(2)}, u32[]{:S(2)}) collective-permute-start(f32[16,2048]{1,0:T(8,128)S(1)} %sub.3), channel_id=1, source_target_pairs={{0,16},{16,32},{32,48},{48,64},{64,80},{80,96},{96,112},{112,128},... | collective-permute-start | bytes 393224 | tf_op jit(solution)/shard_map/ppermute | solution.py:151
  71.9 7.3 %collective-permute-done.3 = f32[16,2048]{1,0:T(8,128)S(1)} collective-permute-done((f32[16,2048]{1,0:T(8,128)S(1)}, f32[16,2048]{1,0:T(8,128)S(1)}, u32[]{:S(2)}, u32[]{:S(2)}) %collective-permute-start.3) | collective-permute-done | bytes 131104 | tf_op jit(solution)/shard_map/ppermute | solution.py:151
  79.2 0.0 all-to-all-done.1
  79.2 0.7 copy.8
  79.8 0.7 copy.9
  (3 shorter events, 0.1 us)
Async XLA Ops:
  0.6 1.1 %copy-start.1 = (f32[1,16,2048]{2,1,0:T(8,128)S(1)}, f32[1,16,2048]{2,1,0:T(8,128)}, u32[]{:S(2)}) copy-start(f32[1,16,2048]{2,1,0:T(8,128)} %param.4) | copy-start | bytes 393220
  0.6 1.1 %copy-start.2 = (f32[16,2048]{1,0:T(8,128)S(1)}, f32[16,2048]{1,0:T(8,128)}, u32[]{:S(2)}) copy-start(f32[16,2048]{1,0:T(8,128)} %diffusivity.1) | copy-start | bytes 393220
  1.7 16.9 %copy-start = (f32[2,16,2048]{2,1,0:T(8,128)S(1)}, f32[2,16,2048]{2,1,0:T(8,128)}, u32[]{:S(2)}) copy-start(f32[2,16,2048]{2,1,0:T(8,128)} %drift.1) | copy-start | bytes 786436
  1.7 16.9 %copy-start.3 = (f32[16,2048]{1,0:T(8,128)S(1)}, f32[16,2048]{1,0:T(8,128)}, u32[]{:S(2)}) copy-start(f32[16,2048]{1,0:T(8,128)} %rate.1) | copy-start | bytes 393220
  1.8 7.4 %collective-permute-start = (f32[64,2048]{1,0:T(8,128)S(1)}, f32[64,2048]{1,0:T(8,128)S(1)}, u32[]{:S(2)}, u32[]{:S(2)}) collective-permute-start(f32[64,2048]{1,0:T(8,128)S(1)} %pad_maximum_fusion), channel_id=1, source_target_pairs={{0,1},{1,0},{2,3},{3,2},{4,5},{5,4},{6,7},{7,6},{8,9},{9,8},{10,11... | collective-permute-start | bytes 1572872 | tf_op jit(solution)/shard_map/ppermute | solution.py:169
  4.5 14.1 %collective-permute-start.1 = (f32[64,2048]{1,0:T(8,128)S(1)}, f32[64,2048]{1,0:T(8,128)S(1)}, u32[]{:S(2)}, u32[]{:S(2)}) collective-permute-start(f32[64,2048]{1,0:T(8,128)S(1)} %pad_maximum_fusion), channel_id=1, source_target_pairs={{0,15},{1,2},{2,1},{3,4},{4,3},{5,6},{6,5},{7,8},{8,7},{9,10},{10,... | collective-permute-start | bytes 1572872 | tf_op jit(solution)/shard_map/ppermute | solution.py:168
  23.1 30.6 %all-to-all-start = ((f32[32,8,128]{2,1,0:T(8,128)}), f32[32,8,128]{2,1,0:T(8,128)S(1)}, u32[]{:S(2)}, u32[]{:S(2)}) async-start(f32[32,8,128]{2,1,0:T(8,128)} %get-tuple-element.5), calls=%async_computation | async-start | bytes 262144 | tf_op jit(solution)/shard_map/all_to_all | solution.py:175
  54.4 24.7 %all-to-all-start.1 = ((f32[32,8,128]{2,1,0:T(8,128)}), f32[32,8,128]{2,1,0:T(8,128)S(1)}, u32[]{:S(2)}, u32[]{:S(2)}) async-start(f32[32,8,128]{2,1,0:T(8,128)} %coarse_solve.1), calls=%async_computation.1 | async-start | bytes 262144 | tf_op jit(solution)/shard_map/all_to_all | solution.py:177
  58.3 11.6 %collective-permute-start.2 = (f32[16,2048]{1,0:T(8,128)S(1)}, f32[16,2048]{1,0:T(8,128)S(1)}, u32[]{:S(2)}, u32[]{:S(2)}) collective-permute-start(f32[16,2048]{1,0:T(8,128)S(1)} %get-tuple-element.6), channel_id=1, source_target_pairs={{0,16},{16,32},{32,48},{48,64},{64,80},{80,96},{96,112},{112,128},... | collective-permute-start | bytes 393224 | tf_op jit(solution)/shard_map/ppermute | solution.py:151
  70.0 9.2 %collective-permute-start.3 = (f32[16,2048]{1,0:T(8,128)S(1)}, f32[16,2048]{1,0:T(8,128)S(1)}, u32[]{:S(2)}, u32[]{:S(2)}) collective-permute-start(f32[16,2048]{1,0:T(8,128)S(1)} %sub.3), channel_id=1, source_target_pairs={{0,16},{16,32},{32,48},{48,64},{64,80},{80,96},{96,112},{112,128},... | collective-permute-start | bytes 393224 | tf_op jit(solution)/shard_map/ppermute | solution.py:151

commit v3 on v2

--- a/solution.py
+++ b/solution.py
@@ -47,7 +47,7 @@
 
 
 def propagate_kernel(
-    parity, cells, drift, diffusivity, rate, inner, outer, second_out, first_out, term_out, rows, coef_rows, state, other, coefs
+    parity, cells, drift, diffusivity, rate, outer, inner, second_out, first_out, term_out, rows, coef_rows, state, other, coefs
 ):
     height, width = cells.shape
     tiles = width // 128
@@ -95,7 +95,7 @@
             term_out[r * tiles + c] = second_out[part] - jnp.exp(-rate[part]) * first_out[part]
 
 
-def propagate(parity, cells, drift, diffusivity, rate, inner, outer):
+def propagate(parity, cells, drift, diffusivity, rate, outer, inner):
     height, width = cells.shape
     tiles = height // 8 * (width // 128)
     shape = lambda *s: jax.ShapeDtypeStruct(s, jnp.float32)
@@ -112,7 +112,7 @@
         in_specs=[pl.BlockSpec(memory_space=pltpu.SMEM)] + [pl.BlockSpec(memory_space=pltpu.VMEM)] * 6,
         compiler_params=pltpu.CompilerParams(vmem_limit_bytes=32 * 1024 * 1024),
         name="propagate",
-    )(parity, cells, drift, diffusivity, rate, inner, outer)
+    )(parity, cells, drift, diffusivity, rate, outer, inner)
 
 
 def solve_kernel(terms, rate, points):
@@ -163,18 +163,19 @@
 def shards(cstates, drift, diffusivity, coarse_rate):
     cells = cstates[0]
     height, width = cells.shape
-    message = jnp.concatenate([cells, drift[0], drift[1], diffusivity], axis=0)
+    message = jnp.concatenate([cells, drift.reshape(-1, width), diffusivity], axis=0)
     strips = lax.axis_size("space")
+    inner = lax.ppermute(message, "space", [(i, i ^ 1) for i in range(strips)])
     outer = lax.ppermute(message, "space", [(i, (((i + 1) ^ 1) - 1) % strips) for i in range(strips)])
-    inner = lax.ppermute(message, "space", [(i, i ^ 1) for i in range(strips)])
     parity = (lax.axis_index("space") % 2).reshape(1)
-    second, first, term = propagate(parity, cells, drift, diffusivity, coarse_rate, inner, outer)
+    second, first, term = propagate(parity, cells, drift, diffusivity, coarse_rate, outer, inner)
     rate = lax.dynamic_index_in_dim(to_tiles(coarse_rate), lax.axis_index("tm"), 0, keepdims=False)
-    ahead = passed_along(second, "tm", 1) - first
-    residual = passed_along(ahead, "tm", 1)
     terms = lax.all_to_all(term, "tm", 0, 0, tiled=True)
+    moved = passed_along(second, "tm", 1)
+    terms, moved = lax.optimization_barrier((terms, moved))
     points = coarse_solve(terms, rate)
     points = lax.all_to_all(points, "tm", 0, 0, tiled=True)
+    residual = passed_along(moved - first, "tm", 1)
     cpoints = from_tiles(points, height, width)
     return cpoints[None], residual[None]
 

time: 80.9 us -> 76.6 us (0.947)
  the two profiles are of different devices: /device:TPU:7 before, /device:TPU:16 now
where the time goes in v3:
time: 76.6 us; the launch traced here: 76.3 us
  starting transfers between devices  35.7 us (47%)
  waiting for transfers between devices  32 us (42%)
  Pallas kernels  5.23 us (7%)
  local copies, waits for them, and re-layouts  1.33 us (2%)
  other arithmetic  1.16 us (2%)
  between operations  0.77 us (1%)
    all_to_all x1, starting transfers between devices, shards(): terms = lax.all_to_all(term, 'tm', 0, 0, tiled=True)  16.2 us
    ppermute x2, waiting for transfers between devices, passed_along(): lax.ppermute(value, axis, [(i, (i + steps) % count) for i in range(count)])  13 us
    ppermute x1, waiting for transfers between devices, shards(): lax.ppermute(message, 'space', [(i, ((i + 1 ^ 1) - 1) % strips) for i in...  8.29 us
    ppermute x2, starting transfers between devices, passed_along(): lax.ppermute(value, axis, [(i, (i + steps) % count) for i in range(count)])  7.4 us
    all_to_all x1, starting transfers between devices, shards(): points = lax.all_to_all(points, 'tm', 0, 0, tiled=True)  6.35 us
    all_to_all x1, waiting for transfers between devices, shards(): points = lax.all_to_all(points, 'tm', 0, 0, tiled=True)  5.91 us
    all_to_all x1, waiting for transfers between devices, shards(): terms = lax.all_to_all(term, 'tm', 0, 0, tiled=True)  4.81 us
    pallas_call x1, Pallas kernels, propagate(): pl.pallas_call(propagate_kernel, out_shape=(shape(height, width), shape(h...  4.53 us
  transfers between devices with their start and end apart: 6, of which 5 were waited for; matrix products, arithmetic and copies ran while one was open for 0% of the time, Pallas kernels for 0%

profile of v3, /device:TPU:16, one launch (start us, length us, event | category | flops | bytes accessed | tf_op | source)
XLA Modules:
  0.0 76.3 jit_solution(14952799512716338280)
XLA Ops:
  0.6 0.0 copy-start
  0.6 0.0 copy-start.1
  0.7 0.0 copy-start.2
  0.7 0.0 copy-start.3
  0.7 1.1 %pad_maximum_fusion = f32[64,2048]{1,0:T(8,128)S(1)} fusion(f32[16,2048]{1,0:T(8,128)} %diffusivity.1, f32[32,2048]{1,0:T(8,128)} %bitcast.16, f32[16,2048]{1,0:T(8,128)} %bitcast.17), kind=kLoop, calls=%fused_computation | loop fusion | flops 262144 | bytes 1048576 | tf_op jit(solution)/shard_map/concatenate | solution.py:166
  1.8 3.9 %collective-permute-start = (f32[64,2048]{1,0:T(8,128)S(1)}, f32[64,2048]{1,0:T(8,128)S(1)}, u32[]{:S(2)}, u32[]{:S(2)}) collective-permute-start(f32[64,2048]{1,0:T(8,128)S(1)} %pad_maximum_fusion), channel_id=1, source_target_pairs={{0,15},{1,2},{2,1},{3,4},{4,3},{5,6},{6,5},{7,8},{8,7},{9,10},{10,... | collective-permute-start | bytes 1572872 | tf_op jit(solution)/shard_map/ppermute | solution.py:169
  5.7 1.9 %collective-permute-start.1 = (f32[64,2048]{1,0:T(8,128)S(1)}, f32[64,2048]{1,0:T(8,128)S(1)}, u32[]{:S(2)}, u32[]{:S(2)}) collective-permute-start(f32[64,2048]{1,0:T(8,128)S(1)} %pad_maximum_fusion), channel_id=1, source_target_pairs={{0,1},{1,0},{2,3},{3,2},{4,5},{5,4},{6,7},{7,6},{8,9},{9,8},{10,11... | collective-permute-start | bytes 1572872 | tf_op jit(solution)/shard_map/ppermute | solution.py:168
  7.6 8.3 %collective-permute-done.outer = f32[64,2048]{1,0:T(8,128)S(1)} collective-permute-done((f32[64,2048]{1,0:T(8,128)S(1)}, f32[64,2048]{1,0:T(8,128)S(1)}, u32[]{:S(2)}, u32[]{:S(2)}) %collective-permute-start) | collective-permute-done | bytes 524320 | tf_op jit(solution)/shard_map/ppermute | solution.py:169
  15.9 0.0 collective-permute-done.1.inner
  15.9 0.0 copy-done
  15.9 0.0 copy-done.1
  15.9 0.0 copy-done.2
  16.0 0.0 copy-done.3
  16.0 4.5 %propagate.1 = (f32[16,2048]{1,0:T(8,128)S(1)}, f32[16,2048]{1,0:T(8,128)S(1)}, f32[32,8,128]{2,1,0:T(8,128)}) custom-call(s32[1]{0:T(128)} %bitcast.parity, f32[16,2048]{1,0:T(8,128)S(1)} %bitcast.18, f32[2,16,2048]{2,1,0:T(8,128)S(1)} %copy-done, f32[16,2048]{1,0:T(8,128)S(1)} %copy-done.2, f32[16,2048]{1,0:T(8,128)S(1)} %copy-done.3, ...), custom_call_target="tpu_custom_call" | custom-call | tf_op jit(solution)/shard_map/propagate/pallas_call | solution.py:102
  20.5 16.2 %all-to-all-start = ((f32[32,8,128]{2,1,0:T(8,128)}), f32[32,8,128]{2,1,0:T(8,128)S(1)}, u32[]{:S(2)}, u32[]{:S(2)}) async-start(f32[32,8,128]{2,1,0:T(8,128)} %get-tuple-element.7), calls=%async_computation | async-start | bytes 262144 | tf_op jit(solution)/shard_map/all_to_all | solution.py:173
  36.7 3.7 %collective-permute-start.2 = (f32[16,2048]{1,0:T(8,128)S(1)}, f32[16,2048]{1,0:T(8,128)S(1)}, u32[]{:S(2)}, u32[]{:S(2)}) collective-permute-start(f32[16,2048]{1,0:T(8,128)S(1)} %get-tuple-element.8), channel_id=1, source_target_pairs={{0,16},{16,32},{32,48},{48,64},{64,80},{80,96},{96,112},{112,128},... | collective-permute-start | bytes 393224 | tf_op jit(solution)/shard_map/ppermute | solution.py:151
  40.4 6.3 %collective-permute-done.2 = f32[16,2048]{1,0:T(8,128)S(1)} collective-permute-done((f32[16,2048]{1,0:T(8,128)S(1)}, f32[16,2048]{1,0:T(8,128)S(1)}, u32[]{:S(2)}, u32[]{:S(2)}) %collective-permute-start.2) | collective-permute-done | bytes 131104 | tf_op jit(solution)/shard_map/ppermute | solution.py:151
  46.7 4.8 %all-to-all-done.terms = f32[32,8,128]{2,1,0:T(8,128)S(1)} async-done(((f32[32,8,128]{2,1,0:T(8,128)}), f32[32,8,128]{2,1,0:T(8,128)S(1)}, u32[]{:S(2)}, u32[]{:S(2)}) %all-to-all-start) | async-done | bytes 131104 | tf_op jit(solution)/shard_map/all_to_all | solution.py:173
  51.5 0.7 coarse_solve.1
  52.2 6.3 %all-to-all-start.1 = ((f32[32,8,128]{2,1,0:T(8,128)}), f32[32,8,128]{2,1,0:T(8,128)S(1)}, u32[]{:S(2)}, u32[]{:S(2)}) async-start(f32[32,8,128]{2,1,0:T(8,128)} %coarse_solve.1), calls=%async_computation.1 | async-start | bytes 262144 | tf_op jit(solution)/shard_map/all_to_all | solution.py:177
  58.6 3.7 %collective-permute-start.3 = (f32[16,2048]{1,0:T(8,128)S(1)}, f32[16,2048]{1,0:T(8,128)S(1)}, u32[]{:S(2)}, u32[]{:S(2)}) collective-permute-start(f32[16,2048]{1,0:T(8,128)S(1)} %sub.3), channel_id=1, source_target_pairs={{0,16},{16,32},{32,48},{48,64},{64,80},{80,96},{96,112},{112,128},... | collective-permute-start | bytes 393224 | tf_op jit(solution)/shard_map/ppermute | solution.py:151
  62.3 6.7 %collective-permute-done.3 = f32[16,2048]{1,0:T(8,128)S(1)} collective-permute-done((f32[16,2048]{1,0:T(8,128)S(1)}, f32[16,2048]{1,0:T(8,128)S(1)}, u32[]{:S(2)}, u32[]{:S(2)}) %collective-permute-start.3) | collective-permute-done | bytes 131104 | tf_op jit(solution)/shard_map/ppermute | solution.py:151
  69.1 5.9 %all-to-all-done.1 = f32[32,8,128]{2,1,0:T(8,128)S(1)} async-done(((f32[32,8,128]{2,1,0:T(8,128)}), f32[32,8,128]{2,1,0:T(8,128)S(1)}, u32[]{:S(2)}, u32[]{:S(2)}) %all-to-all-start.1) | async-done | bytes 131104 | tf_op jit(solution)/shard_map/all_to_all | solution.py:177
  75.0 0.7 copy.8
  75.6 0.7 copy.9
  (2 shorter events, 0.0 us)
Async XLA Ops:
  0.6 15.3 %copy-start = (f32[2,16,2048]{2,1,0:T(8,128)S(1)}, f32[2,16,2048]{2,1,0:T(8,128)}, u32[]{:S(2)}) copy-start(f32[2,16,2048]{2,1,0:T(8,128)} %drift.1) | copy-start | bytes 786436
  0.6 15.3 %copy-start.1 = (f32[1,16,2048]{2,1,0:T(8,128)S(1)}, f32[1,16,2048]{2,1,0:T(8,128)}, u32[]{:S(2)}) copy-start(f32[1,16,2048]{2,1,0:T(8,128)} %param.4) | copy-start | bytes 393220
  0.7 15.3 %copy-start.2 = (f32[16,2048]{1,0:T(8,128)S(1)}, f32[16,2048]{1,0:T(8,128)}, u32[]{:S(2)}) copy-start(f32[16,2048]{1,0:T(8,128)} %diffusivity.1) | copy-start | bytes 393220
  0.7 15.3 %copy-start.3 = (f32[16,2048]{1,0:T(8,128)S(1)}, f32[16,2048]{1,0:T(8,128)}, u32[]{:S(2)}) copy-start(f32[16,2048]{1,0:T(8,128)} %rate.1) | copy-start | bytes 393220
  1.8 14.1 %collective-permute-start = (f32[64,2048]{1,0:T(8,128)S(1)}, f32[64,2048]{1,0:T(8,128)S(1)}, u32[]{:S(2)}, u32[]{:S(2)}) collective-permute-start(f32[64,2048]{1,0:T(8,128)S(1)} %pad_maximum_fusion), channel_id=1, source_target_pairs={{0,15},{1,2},{2,1},{3,4},{4,3},{5,6},{6,5},{7,8},{8,7},{9,10},{10,... | collective-permute-start | bytes 1572872 | tf_op jit(solution)/shard_map/ppermute | solution.py:169
  5.7 10.2 %collective-permute-start.1 = (f32[64,2048]{1,0:T(8,128)S(1)}, f32[64,2048]{1,0:T(8,128)S(1)}, u32[]{:S(2)}, u32[]{:S(2)}) collective-permute-start(f32[64,2048]{1,0:T(8,128)S(1)} %pad_maximum_fusion), channel_id=1, source_target_pairs={{0,1},{1,0},{2,3},{3,2},{4,5},{5,4},{6,7},{7,6},{8,9},{9,8},{10,11... | collective-permute-start | bytes 1572872 | tf_op jit(solution)/shard_map/ppermute | solution.py:168
  20.5 31.0 %all-to-all-start = ((f32[32,8,128]{2,1,0:T(8,128)}), f32[32,8,128]{2,1,0:T(8,128)S(1)}, u32[]{:S(2)}, u32[]{:S(2)}) async-start(f32[32,8,128]{2,1,0:T(8,128)} %get-tuple-element.7), calls=%async_computation | async-start | bytes 262144 | tf_op jit(solution)/shard_map/all_to_all | solution.py:173
  36.7 10.0 %collective-permute-start.2 = (f32[16,2048]{1,0:T(8,128)S(1)}, f32[16,2048]{1,0:T(8,128)S(1)}, u32[]{:S(2)}, u32[]{:S(2)}) collective-permute-start(f32[16,2048]{1,0:T(8,128)S(1)} %get-tuple-element.8), channel_id=1, source_target_pairs={{0,16},{16,32},{32,48},{48,64},{64,80},{80,96},{96,112},{112,128},... | collective-permute-start | bytes 393224 | tf_op jit(solution)/shard_map/ppermute | solution.py:151
  52.2 22.7 %all-to-all-start.1 = ((f32[32,8,128]{2,1,0:T(8,128)}), f32[32,8,128]{2,1,0:T(8,128)S(1)}, u32[]{:S(2)}, u32[]{:S(2)}) async-start(f32[32,8,128]{2,1,0:T(8,128)} %coarse_solve.1), calls=%async_computation.1 | async-start | bytes 262144 | tf_op jit(solution)/shard_map/all_to_all | solution.py:177
  58.6 10.4 %collective-permute-start.3 = (f32[16,2048]{1,0:T(8,128)S(1)}, f32[16,2048]{1,0:T(8,128)S(1)}, u32[]{:S(2)}, u32[]{:S(2)}) collective-permute-start(f32[16,2048]{1,0:T(8,128)S(1)} %sub.3), channel_id=1, source_target_pairs={{0,16},{16,32},{32,48},{48,64},{64,80},{80,96},{96,112},{112,128},... | collective-permute-start | bytes 393224 | tf_op jit(solution)/shard_map/ppermute | solution.py:151

commit v4 on v3

v4 whole, which is shorter than its diff:
```python
import jax
import jax.numpy as jnp
from jax import lax
from jax.experimental import pallas as pl
from jax.experimental.pallas import tpu as pltpu
from jax.sharding import PartitionSpec as P

M = 8
nonlinear_weight = 0.05


def store_kernel(value, out, sem):
    copy = pltpu.make_async_copy(value, out, sem)
    copy.start()
    copy.wait()


def store(value):
    return pl.pallas_call(
        store_kernel,
        out_shape=jax.ShapeDtypeStruct(value.shape, jnp.float32),
        in_specs=[pl.BlockSpec(memory_space=pltpu.VMEM)],
        out_specs=pl.BlockSpec(memory_space=pl.ANY),
        scratch_shapes=[pltpu.SemaphoreType.DMA],
        compiler_params=pltpu.CompilerParams(vmem_limit_bytes=2 * 1024 * 1024),
        name="store",
    )(value)


def next_cell(u, above, below, right, left, coefs):
    spread = coefs[2] * ((above + below) + (right + left))
    along = (coefs[0] + (0.5 * nonlinear_weight) * u) * (right - left)
    across = coefs[1] * (above - below)
    return ((coefs[3] * u + spread) - along) - across


def load_state(strips, rows):
    tiles = rows.shape[0]
    for c in range(tiles):
        for k, strip in enumerate(strips):
            for r in range(2):
                rows[c, k * 16 + r * 8 : k * 16 + r * 8 + 8] = strip[r * tiles + c]


def load_coefs(strips, coef_rows):
    tiles = coef_rows.shape[1]
    for c in range(tiles):
        for k, strip in enumerate(strips):
            for r in range(2):
                place = slice(k * 16 + r * 8, k * 16 + r * 8 + 8)
                parts = [strip[(2 * f + r) * tiles + c] for f in (1, 2, 3)]
                coef_rows[0, c, place] = 0.5 * parts[0]
                coef_rows[1, c, place] = 0.5 * parts[1]
                coef_rows[2, c, place] = parts[2]
                coef_rows[3, c, place] = 1.0 - 4.0 * parts[2]


def near_kernel(parity, own, inner, history, first_half, rows, coef_rows, state, other, coefs):
    tiles, blocks = state.shape[0], state.shape[1]
    lane = lax.broadcasted_iota(jnp.int32, (8, 128), 1)
    is_last, is_first = lane == 127, lane == 0

    def one(src, dst):
        for i in range(blocks):
            to_left = lambda c: pltpu.roll(src[c % tiles, i], 127, 1)
            to_right = lambda c: pltpu.roll(src[c % tiles, i], 1, 1)
            ahead, behind, here = to_left(0), to_right(-1), to_right(0)
            for c in range(tiles):
                u = src[c, i]
                above = src[c, i + 1] if i + 1 < blocks else pltpu.roll(src[c, 0], 7, 0)
                below = src[c, i - 1] if i > 0 else pltpu.roll(src[c, blocks - 1], 1, 0)
                following = to_left(c + 1)
                right = jnp.where(is_last, following, ahead)
                left = jnp.where(is_first, behind, here)
                ahead, behind, here = following, here, to_right(c + 1)
                dst[c, i] = next_cell(u, above, below, right, left, [coefs[f, c, i] for f in range(4)])

    def run(strips, inner_is_after):
        load_coefs(strips, coef_rows)
        load_state(strips, rows)
        for c in range(tiles):
            for i in range(blocks):
                place = pl.ds(i, 8, stride=blocks)
                state[c, i] = rows[c, place, :]
                for f in range(4):
                    coefs[f, c, i] = coef_rows[f, c, place, :]

        def group(g, carry):
            for j in range(blocks):
                src, dst = (state, other) if j % 2 == 0 else (other, state)
                for w in range(2):
                    sub, block = divmod(j + w, blocks)
                    if inner_is_after:
                        row = (block, g + sub)
                    else:
                        row = (blocks - 1 - block, 7 - g - sub)
                    for c in range(tiles):
                        history[blocks * g + j, w, c : c + 1] = src[c, row[0], pl.ds(row[1], 1), :]
                one(src, dst)

            @pl.when(g == M // blocks - 1)
            def _():
                for c in range(tiles):
                    for i in range(blocks):
                        rows[c, pl.ds(i, 8, stride=blocks), :] = state[c, i]
                start = M if inner_is_after else 2 * M
                for c in range(tiles):
                    first_half[:, c * 128 : c * 128 + 128] = rows[c, start : start + M]

            return carry

        lax.fori_loop(0, 2 * M // blocks, group, 0)

    @pl.when(parity[0] == 0)
    def _():
        run((own, inner), True)

    @pl.when(parity[0] == 1)
    def _():
        run((inner, own), False)


def near(parity, own, inner):
    height, tiles = 16, own.shape[0] // 8
    width = tiles * 128
    return pl.pallas_call(
        near_kernel,
        out_shape=(
            jax.ShapeDtypeStruct((2 * M, 2, tiles, 128), jnp.float32),
            jax.ShapeDtypeStruct((M, width), jnp.float32),
        ),
        scratch_shapes=[
            pltpu.VMEM((tiles, 2 * height, 128), jnp.float32),
            pltpu.VMEM((4, tiles, 2 * height, 128), jnp.float32),
            pltpu.VMEM((tiles, 4, 8, 128), jnp.float32),
            pltpu.VMEM((tiles, 4, 8, 128), jnp.float32),
            pltpu.VMEM((4, tiles, 4, 8, 128), jnp.float32),
        ],
        in_specs=[pl.BlockSpec(memory_space=pltpu.SMEM)] + [pl.BlockSpec(memory_space=pltpu.VMEM)] * 2,
        compiler_params=pltpu.CompilerParams(vmem_limit_bytes=16 * 1024 * 1024),
        cost_estimate=pl.CostEstimate(flops=0, bytes_accessed=0, transcendentals=0),
        name="near",
    )(parity, own, inner)


def far_kernel(
    parity, own, rate, outer, history, first_half, second_out, first_out, term_out, rows, coef_rows, state, other
):
    tiles = state.shape[0]
    lane = lax.broadcasted_iota(jnp.int32, (8, 128), 1)
    is_last, is_first = lane == 127, lane == 0
    sub = lax.broadcasted_iota(jnp.int32, (8, 128), 0)

    def one(k, src, dst, outer_is_before):
        def column(c):
            c = c % tiles
            even, odd = src[c, 0], src[c, 1]
            joins = [jnp.broadcast_to(history[k, w, c : c + 1], (8, 128)) for w in range(2)]
            if outer_is_before:
                even_on = jnp.where(sub == 7, joins[0], pltpu.roll(even, 7, 0))
                odd_on = jnp.where(sub == 7, joins[1], pltpu.roll(odd, 7, 0))
                cells = [(odd, even_on, even), (even_on, odd_on, odd)]
            else:
                even_on = jnp.where(sub == 0, joins[1], pltpu.roll(even, 1, 0))
                odd_on = jnp.where(sub == 0, joins[0], pltpu.roll(odd, 1, 0))
                cells = [(odd_on, even, even_on), (even, odd, odd_on)]
            return cells, [pltpu.roll(u, 127, 1) for u, _, _ in cells], [pltpu.roll(u, 1, 1) for u, _, _ in cells]

        behind, here = column(-1), column(0)
        top = k + 1 if outer_is_before else 2 * M - 1 - k
        for c in range(tiles):
            ahead = column(c + 1)
            for i in range(2):
                u, above, below = here[0][i]
                right = jnp.where(is_last, ahead[1][i], here[1][i])
                left = jnp.where(is_first, behind[2][i], here[2][i])
                place = pl.ds(top + i, 8, stride=2)
                dst[c, i] = next_cell(u, above, below, right, left, [coef_rows[f, c, place, :] for f in range(4)])
            behind, here = here, ahead

    def unfold():
        for c in range(tiles):
            for i in range(2):
                rows[c, pl.ds(i, 8, stride=2), :] = state[c, i]

    def run(strips, outer_is_before):
        load_coefs(strips, coef_rows)
        load_state((outer,), rows)
        for c in range(tiles):
            for i in range(2):
                state[c, i] = rows[c, pl.ds(i, 8, stride=2), :]

        def pair(h, carry):
            @pl.when(h == M // 2)
            def _():
                unfold()
                for c in range(tiles):
                    cols = slice(c * 128, c * 128 + 128)
                    if outer_is_before:
                        first_out[0:M, cols] = rows[c, M : 2 * M]
                        first_out[M : 2 * M, cols] = first_half[:, cols]
                    else:
                        first_out[0:M, cols] = first_half[:, cols]
                        first_out[M : 2 * M, cols] = rows[c, 0:M]

            one(2 * h, state, other, outer_is_before)
            one(2 * h + 1, other, state, outer_is_before)
            return carry

        lax.fori_loop(0, M, pair, 0)

    @pl.when(parity[0] == 0)
    def _():
        run((outer, own), True)

    @pl.when(parity[0] == 1)
    def _():
        run((own, outer), False)

    unfold()
    for c in range(tiles):
        cols = slice(c * 128, c * 128 + 128)
        second_out[:, cols] = rows[c]
        for r in range(2):
            part = (slice(r * 8, r * 8 + 8), cols)
            term_out[r * tiles + c] = rows[c, r * 8 : r * 8 + 8] - jnp.exp(-rate[part]) * first_out[part]


def far(parity, own, rate, outer, history, first_half):
    height, width = rate.shape
    tiles = width // 128
    shape = lambda *s: jax.ShapeDtypeStruct(s, jnp.float32)
    return pl.pallas_call(
        far_kernel,
        out_shape=(shape(height, width), shape(height, width), shape(2 * tiles, 8, 128)),
        scratch_shapes=[
            pltpu.VMEM((tiles, height, 128), jnp.float32),
            pltpu.VMEM((4, tiles, 2 * height, 128), jnp.float32),
            pltpu.VMEM((tiles, 2, 8, 128), jnp.float32),
            pltpu.VMEM((tiles, 2, 8, 128), jnp.float32),
        ],
        in_specs=[pl.BlockSpec(memory_space=pltpu.SMEM)] + [pl.BlockSpec(memory_space=pltpu.VMEM)] * 5,
        compiler_params=pltpu.CompilerParams(vmem_limit_bytes=16 * 1024 * 1024),
        name="far",
    )(parity, own, rate, outer, history, first_half)


def solve_kernel(terms, rate, points):
    intervals, length = terms.shape[0], 8
    chains = intervals // length
    powers = [jnp.exp(-rate[...])]
    for _ in range(length - 1):
        powers.append(powers[-1] * powers[0])
    sums = [[terms[c * length]] for c in range(chains)]
    for k in range(1, length):
        for c in range(chains):
            sums[c].append(powers[0] * sums[c][-1] + terms[c * length + k])
    jump = powers[-1]
    closing, whole = sums[0][-1], jump
    for c in range(1, chains):
        closing = jump * closing + sums[c][-1]
        whole = whole * jump
    carry = closing / (1.0 - whole)
    for c in range(chains):
        for k in range(length):
            points[(c * length + k + 2) % intervals] = powers[k] * carry + sums[c][k]
        carry = jump * carry + sums[c][-1]


def coarse_solve(terms, rate):
    return pl.pallas_call(
        solve_kernel,
        out_shape=jax.ShapeDtypeStruct(terms.shape, jnp.float32),
        compiler_params=pltpu.CompilerParams(vmem_limit_bytes=2 * 1024 * 1024),
        name="coarse_solve",
    )(terms, rate)


def passed_along(value, axis, steps):
    count = lax.axis_size(axis)
    return lax.ppermute(value, axis, [(i, (i + steps) % count) for i in range(count)])


def to_tiles(value):
    height, width = value.shape
    return value.reshape(height // 8, 8, width // 128, 128).transpose(0, 2, 1, 3).reshape(-1, 8, 128)


def from_tiles(value, height, width):
    return value.reshape(height // 8, width // 128, 8, 128).transpose(0, 2, 1, 3).reshape(height, width)


def shards(cstates, drift, diffusivity, coarse_rate):
    cells = cstates[0]
    height, width = cells.shape
    parts = [to_tiles(cells), to_tiles(drift.reshape(-1, width)), to_tiles(diffusivity)]
    message = jnp.concatenate(parts)
    strips = lax.axis_size("space")
    inner = lax.ppermute(message, "space", [(i, i ^ 1) for i in range(strips)])
    outer = lax.ppermute(jnp.concatenate(parts + [jnp.zeros((1, 8, 128), jnp.float32)]), "space", [(i, (((i + 1) ^ 1) - 1) % strips) for i in range(strips)])
    parity = (lax.axis_index("space") % 2).reshape(1)
    history, first_half = near(parity, message, inner)
    second, first, term = far(parity, message, coarse_rate, outer, history, first_half)
    rate = lax.dynamic_index_in_dim(to_tiles(coarse_rate), lax.axis_index("tm"), 0, keepdims=False)
    terms = lax.all_to_all(term, "tm", 0, 0, tiled=True)
    moved = passed_along(second, "tm", 1)
    terms, moved = lax.optimization_barrier((terms, moved))
    points = coarse_solve(terms, rate)
    points = lax.all_to_all(points, "tm", 0, 0, tiled=True)
    residual = store(passed_along(moved - first, "tm", 1))
    cpoints = from_tiles(points, height, width)
    return cpoints[None], residual[None]


def solution(mesh):
    placed = (P("tm", "space", None), P(None, "space", None), P("space", None), P("space", None))
    return jax.shard_map(
        shards,
        mesh=mesh,
        in_specs=placed,
        out_specs=(P("tm", "space", None), P("tm", "space", None)),
        check_vma=False,
    )
```

time: 76.6 us -> 75.3 us (0.983)
  the two profiles are of different devices: /device:TPU:16 before, /device:TPU:6 now
where the time goes in v4:
time: 75.3 us; the launch traced here: 74.9 us
  starting transfers between devices  37.5 us (50%)
  waiting for transfers between devices  26.9 us (36%)
  Pallas kernels  7.67 us (10%)
  other arithmetic  1.35 us (2%)
  between operations  0.81 us (1%)
    ppermute x2, waiting for transfers between devices, passed_along(): lax.ppermute(value, axis, [(i, (i + steps) % count) for i in range(count)])  19.2 us
    all_to_all x1, starting transfers between devices, shards(): terms = lax.all_to_all(term, 'tm', 0, 0, tiled=True)  15.6 us
    all_to_all x1, starting transfers between devices, shards(): points = lax.all_to_all(points, 'tm', 0, 0, tiled=True)  7.5 us
    ppermute x2, starting transfers between devices, passed_along(): lax.ppermute(value, axis, [(i, (i + steps) % count) for i in range(count)])  7.4 us
    ppermute x1, starting transfers between devices, shards(): inner = lax.ppermute(message, 'space', [(i, i ^ 1) for i in range(strips)])  4.86 us
    all_to_all x1, waiting for transfers between devices, shards(): points = lax.all_to_all(points, 'tm', 0, 0, tiled=True)  3.98 us
    pallas_call x1, Pallas kernels, far(): pl.pallas_call(far_kernel, out_shape=(shape(height, width), shape(height,...  3.27 us
    pallas_call x1, Pallas kernels, near(): pl.pallas_call(near_kernel, out_shape=(jax.ShapeDtypeStruct((2 * M, 2, ti...  3.04 us
  transfers between devices with their start and end apart: 6, of which 5 were waited for; matrix products, arithmetic and copies ran while one was open for 0% of the time, Pallas kernels for 5%

profile of v4, /device:TPU:6, one launch (start us, length us, event | category | flops | bytes accessed | tf_op | source)
XLA Modules:
  0.0 74.9 jit_solution(2909785503859248215)
XLA Ops:
  0.6 0.0 copy-start.1
  0.7 0.0 copy-start.2
  0.7 0.0 copy-start.3
  0.7 1.3 %maximum_maximum_fusion = f32[129,8,128]{2,1,0:T(8,128)S(1)} fusion(f32[32,8,128]{2,1,0:T(8,128)} %bitcast.34, f32[64,8,128]{2,1,0:T(8,128)} %bitcast.31, f32[32,8,128]{2,1,0:T(8,128)} %bitcast.36, f32[129]{0:T(256)S(1)} %pad.3.clone), kind=kLoop, calls=%fused_computation | loop fusion | flops 396288 | bytes 1053188 | tf_op jit(solution)/shard_map/concatenate | solution.py:300
  2.0 2.2 %collective-permute-start = (f32[129,8,128]{2,1,0:T(8,128)S(1)}, f32[129,8,128]{2,1,0:T(8,128)S(1)}, u32[]{:S(2)}, u32[]{:S(2)}) collective-permute-start(f32[129,8,128]{2,1,0:T(8,128)S(1)} %maximum_maximum_fusion), channel_id=1, source_target_pairs={{0,15},{1,2},{2,1},{3,4},{4,3},{5,6},{6,5},{7,8},{8,7},{9,10},{10,... | collective-permute-start | bytes 1585160 | tf_op jit(solution)/shard_map/ppermute | solution.py:300
  4.2 0.0 copy-done.1
  4.2 0.0 copy-done.2
  4.2 0.0 copy-done.3
  4.2 4.9 %collective-permute-start.1 = (f32[128,8,128]{2,1,0:T(8,128)S(1)}, f32[128,8,128]{2,1,0:T(8,128)S(1)}, u32[]{:S(2)}, u32[]{:S(2)}) collective-permute-start(f32[128,8,128]{2,1,0:T(8,128)S(1)} %pad_maximum_fusion.own), channel_id=1, source_target_pairs={{0,1},{1,0},{2,3},{3,2},{4,5},{5,4},{6,7},{7,6},{8,9},{9,8},{10,11... | collective-permute-start | bytes 1572872 | tf_op jit(solution)/shard_map/ppermute | solution.py:299
  9.1 1.5 %collective-permute-done.1.inner = f32[128,8,128]{2,1,0:T(8,128)S(1)} collective-permute-done((f32[128,8,128]{2,1,0:T(8,128)S(1)}, f32[128,8,128]{2,1,0:T(8,128)S(1)}, u32[]{:S(2)}, u32[]{:S(2)}) %collective-permute-start.1) | collective-permute-done | bytes 524320 | tf_op jit(solution)/shard_map/ppermute | solution.py:299
  10.6 0.0 copy-start
  10.6 3.0 %near.1 = (f32[16,2,16,128]{3,2,1,0:T(8,128)S(1)}, f32[8,2048]{1,0:T(8,128)S(1)}) custom-call(s32[1]{0:T(128)} %bitcast.parity, f32[128,8,128]{2,1,0:T(8,128)S(1)} %pad_maximum_fusion.own, f32[128,8,128]{2,1,0:T(8,128)S(1)} %collective-permute-done.1.inner), custom_call_target="tpu_custom_call" | custom-call | tf_op jit(solution)/shard_map/near/pallas_call | solution.py:126
  13.7 0.0 collective-permute-done.outer
  13.7 0.0 copy-done
  13.7 3.3 %far.1 = (f32[16,2048]{1,0:T(8,128)S(1)}, f32[16,2048]{1,0:T(8,128)S(1)}, f32[32,8,128]{2,1,0:T(8,128)}) custom-call(s32[1]{0:T(128)} %bitcast.parity, f32[128,8,128]{2,1,0:T(8,128)S(1)} %pad_maximum_fusion.own, f32[16,2048]{1,0:T(8,128)S(1)} %copy-done, f32[129,8,128]{2,1,0:T(8,128)S(1)} %collective-permute-done.outer, ...), custom_call_target="tpu_custom_call" | custom-call | tf_op jit(solution)/shard_map/far/pallas_call | solution.py:233
  17.0 15.6 %all-to-all-start = ((f32[32,8,128]{2,1,0:T(8,128)}), f32[32,8,128]{2,1,0:T(8,128)S(1)}, u32[]{:S(2)}, u32[]{:S(2)}) async-start(f32[32,8,128]{2,1,0:T(8,128)} %get-tuple-element.11), calls=%async_computation | async-start | bytes 262144 | tf_op jit(solution)/shard_map/all_to_all | solution.py:305
  32.6 3.7 %collective-permute-start.2 = (f32[16,2048]{1,0:T(8,128)S(1)}, f32[16,2048]{1,0:T(8,128)S(1)}, u32[]{:S(2)}, u32[]{:S(2)}) collective-permute-start(f32[16,2048]{1,0:T(8,128)S(1)} %get-tuple-element.12), channel_id=1, source_target_pairs={{0,16},{16,32},{32,48},{48,64},{64,80},{80,96},{96,112},{112,128},... | collective-permute-start | bytes 393224 | tf_op jit(solution)/shard_map/ppermute | solution.py:281
  36.3 9.8 %collective-permute-done.2 = f32[16,2048]{1,0:T(8,128)S(1)} collective-permute-done((f32[16,2048]{1,0:T(8,128)S(1)}, f32[16,2048]{1,0:T(8,128)S(1)}, u32[]{:S(2)}, u32[]{:S(2)}) %collective-permute-start.2) | collective-permute-done | bytes 131104 | tf_op jit(solution)/shard_map/ppermute | solution.py:281
  46.1 2.2 %all-to-all-done.terms = f32[32,8,128]{2,1,0:T(8,128)S(1)} async-done(((f32[32,8,128]{2,1,0:T(8,128)}), f32[32,8,128]{2,1,0:T(8,128)S(1)}, u32[]{:S(2)}, u32[]{:S(2)}) %all-to-all-start) | async-done | bytes 131104 | tf_op jit(solution)/shard_map/all_to_all | solution.py:305
  48.3 0.7 coarse_solve.1
  49.0 7.5 %all-to-all-start.1 = ((f32[32,8,128]{2,1,0:T(8,128)}), f32[32,8,128]{2,1,0:T(8,128)S(1)}, u32[]{:S(2)}, u32[]{:S(2)}) async-start(f32[32,8,128]{2,1,0:T(8,128)} %coarse_solve.1), calls=%async_computation.1 | async-start | bytes 262144 | tf_op jit(solution)/shard_map/all_to_all | solution.py:309
  56.5 3.7 %collective-permute-start.3 = (f32[16,2048]{1,0:T(8,128)S(1)}, f32[16,2048]{1,0:T(8,128)S(1)}, u32[]{:S(2)}, u32[]{:S(2)}) collective-permute-start(f32[16,2048]{1,0:T(8,128)S(1)} %sub.3), channel_id=1, source_target_pairs={{0,16},{16,32},{32,48},{48,64},{64,80},{80,96},{96,112},{112,128},... | collective-permute-start | bytes 393224 | tf_op jit(solution)/shard_map/ppermute | solution.py:281
  60.2 9.4 %collective-permute-done.3.value = f32[16,2048]{1,0:T(8,128)S(1)} collective-permute-done((f32[16,2048]{1,0:T(8,128)S(1)}, f32[16,2048]{1,0:T(8,128)S(1)}, u32[]{:S(2)}, u32[]{:S(2)}) %collective-permute-start.3) | collective-permute-done | bytes 131104 | tf_op jit(solution)/shard_map/ppermute | solution.py:281
  69.6 0.7 store.1
  70.3 4.0 %all-to-all-done.1 = f32[32,8,128]{2,1,0:T(8,128)S(1)} async-done(((f32[32,8,128]{2,1,0:T(8,128)}), f32[32,8,128]{2,1,0:T(8,128)S(1)}, u32[]{:S(2)}, u32[]{:S(2)}) %all-to-all-start.1) | async-done | bytes 131104 | tf_op jit(solution)/shard_map/all_to_all | solution.py:309
  74.3 0.7 copy.7
  (4 shorter events, 0.1 us)
Async XLA Ops:
  0.6 3.5 %copy-start.1 = (f32[2,16,2048]{2,1,0:T(8,128)S(1)}, f32[2,16,2048]{2,1,0:T(8,128)}, u32[]{:S(2)}) copy-start(f32[2,16,2048]{2,1,0:T(8,128)} %param.5) | copy-start | bytes 786436
  0.7 3.5 %copy-start.2 = (f32[16,2048]{1,0:T(8,128)S(1)}, f32[16,2048]{1,0:T(8,128)}, u32[]{:S(2)}) copy-start(f32[16,2048]{1,0:T(8,128)} %param.6) | copy-start | bytes 393220
  0.7 3.5 %copy-start.3 = (f32[1,16,2048]{2,1,0:T(8,128)S(1)}, f32[1,16,2048]{2,1,0:T(8,128)}, u32[]{:S(2)}) copy-start(f32[1,16,2048]{2,1,0:T(8,128)} %param.4) | copy-start | bytes 393220
  2.0 11.7 %collective-permute-start = (f32[129,8,128]{2,1,0:T(8,128)S(1)}, f32[129,8,128]{2,1,0:T(8,128)S(1)}, u32[]{:S(2)}, u32[]{:S(2)}) collective-permute-start(f32[129,8,128]{2,1,0:T(8,128)S(1)} %maximum_maximum_fusion), channel_id=1, source_target_pairs={{0,15},{1,2},{2,1},{3,4},{4,3},{5,6},{6,5},{7,8},{8,7},{9,10},{10,... | collective-permute-start | bytes 1585160 | tf_op jit(solution)/shard_map/ppermute | solution.py:300
  4.2 6.4 %collective-permute-start.1 = (f32[128,8,128]{2,1,0:T(8,128)S(1)}, f32[128,8,128]{2,1,0:T(8,128)S(1)}, u32[]{:S(2)}, u32[]{:S(2)}) collective-permute-start(f32[128,8,128]{2,1,0:T(8,128)S(1)} %pad_maximum_fusion.own), channel_id=1, source_target_pairs={{0,1},{1,0},{2,3},{3,2},{4,5},{5,4},{6,7},{7,6},{8,9},{9,8},{10,11... | collective-permute-start | bytes 1572872 | tf_op jit(solution)/shard_map/ppermute | solution.py:299
  10.6 3.1 %copy-start = (f32[16,2048]{1,0:T(8,128)S(1)}, f32[16,2048]{1,0:T(8,128)}, u32[]{:S(2)}) copy-start(f32[16,2048]{1,0:T(8,128)} %rate.1) | copy-start | bytes 393220
  17.0 31.3 %all-to-all-start = ((f32[32,8,128]{2,1,0:T(8,128)}), f32[32,8,128]{2,1,0:T(8,128)S(1)}, u32[]{:S(2)}, u32[]{:S(2)}) async-start(f32[32,8,128]{2,1,0:T(8,128)} %get-tuple-element.11), calls=%async_computation | async-start | bytes 262144 | tf_op jit(solution)/shard_map/all_to_all | solution.py:305
  32.6 13.5 %collective-permute-start.2 = (f32[16,2048]{1,0:T(8,128)S(1)}, f32[16,2048]{1,0:T(8,128)S(1)}, u32[]{:S(2)}, u32[]{:S(2)}) collective-permute-start(f32[16,2048]{1,0:T(8,128)S(1)} %get-tuple-element.12), channel_id=1, source_target_pairs={{0,16},{16,32},{32,48},{48,64},{64,80},{80,96},{96,112},{112,128},... | collective-permute-start | bytes 393224 | tf_op jit(solution)/shard_map/ppermute | solution.py:281
  49.0 25.3 %all-to-all-start.1 = ((f32[32,8,128]{2,1,0:T(8,128)}), f32[32,8,128]{2,1,0:T(8,128)S(1)}, u32[]{:S(2)}, u32[]{:S(2)}) async-start(f32[32,8,128]{2,1,0:T(8,128)} %coarse_solve.1), calls=%async_computation.1 | async-start | bytes 262144 | tf_op jit(solution)/shard_map/all_to_all | solution.py:309
  56.5 13.1 %collective-permute-start.3 = (f32[16,2048]{1,0:T(8,128)S(1)}, f32[16,2048]{1,0:T(8,128)S(1)}, u32[]{:S(2)}, u32[]{:S(2)}) collective-permute-start(f32[16,2048]{1,0:T(8,128)S(1)} %sub.3), channel_id=1, source_target_pairs={{0,16},{16,32},{32,48},{48,64},{64,80},{80,96},{96,112},{112,128},... | collective-permute-start | bytes 393224 | tf_op jit(solution)/shard_map/ppermute | solution.py:281

commit v5 on v4

--- a/solution.py
+++ b/solution.py
@@ -303,11 +303,11 @@
     second, first, term = far(parity, message, coarse_rate, outer, history, first_half)
     rate = lax.dynamic_index_in_dim(to_tiles(coarse_rate), lax.axis_index("tm"), 0, keepdims=False)
     terms = lax.all_to_all(term, "tm", 0, 0, tiled=True)
-    moved = passed_along(second, "tm", 1)
-    terms, moved = lax.optimization_barrier((terms, moved))
+    second = passed_along(second, "tm", 2)
+    first = passed_along(first, "tm", 1)
     points = coarse_solve(terms, rate)
     points = lax.all_to_all(points, "tm", 0, 0, tiled=True)
-    residual = store(passed_along(moved - first, "tm", 1))
+    residual = second - first
     cpoints = from_tiles(points, height, width)
     return cpoints[None], residual[None]
 

time: 75.3 us -> 73.8 us (0.980)
  the two profiles are of different devices: /device:TPU:6 before, /device:TPU:7 now
where the time goes in v5:
time: 73.8 us; the launch traced here: 72.5 us
  starting transfers between devices  34.4 us (47%)
  waiting for transfers between devices  27.5 us (37%)
  Pallas kernels  7.07 us (10%)
  other arithmetic  2 us (3%)
  between operations  0.8 us (1%)
    all_to_all x1, starting transfers between devices, shards(): terms = lax.all_to_all(term, 'tm', 0, 0, tiled=True)  16.2 us
    all_to_all x1, waiting for transfers between devices, shards(): points = lax.all_to_all(points, 'tm', 0, 0, tiled=True)  14.6 us
    all_to_all x1, waiting for transfers between devices, shards(): terms = lax.all_to_all(term, 'tm', 0, 0, tiled=True)  9.15 us
    ppermute x2, starting transfers between devices, passed_along(): lax.ppermute(value, axis, [(i, (i + steps) % count) for i in range(count)])  7.13 us
    ppermute x1, starting transfers between devices, shards(): lax.ppermute(jnp.concatenate(parts + [jnp.zeros((1, 8, 128), jnp.float32)...  5.3 us
    all_to_all x1, starting transfers between devices, shards(): points = lax.all_to_all(points, 'tm', 0, 0, tiled=True)  3.86 us
    pallas_call x1, Pallas kernels, far(): pl.pallas_call(far_kernel, out_shape=(shape(height, width), shape(height,...  3.34 us
    pallas_call x1, Pallas kernels, near(): pl.pallas_call(near_kernel, out_shape=(jax.ShapeDtypeStruct((2 * M, 2, ti...  3.03 us
  transfers between devices with their start and end apart: 6, of which 4 were waited for; matrix products, arithmetic and copies ran while one was open for 1% of the time, Pallas kernels for 5%

profile of v5, /device:TPU:7, one launch (start us, length us, event | category | flops | bytes accessed | tf_op | source)
XLA Modules:
  0.0 72.5 jit_solution(856828339207774742)
XLA Ops:
  0.6 0.0 copy-start.1
  0.7 0.0 copy-start.2
  0.7 0.0 copy-start.3
  0.7 1.3 %maximum_maximum_fusion = f32[129,8,128]{2,1,0:T(8,128)S(1)} fusion(f32[32,8,128]{2,1,0:T(8,128)} %bitcast.35, f32[64,8,128]{2,1,0:T(8,128)} %bitcast.32, f32[32,8,128]{2,1,0:T(8,128)} %bitcast.37, f32[129]{0:T(256)S(1)} %pad.3.clone), kind=kLoop, calls=%fused_computation | loop fusion | flops 396288 | bytes 1053188 | tf_op jit(solution)/shard_map/concatenate | solution.py:300
  2.0 5.3 %collective-permute-start = (f32[129,8,128]{2,1,0:T(8,128)S(1)}, f32[129,8,128]{2,1,0:T(8,128)S(1)}, u32[]{:S(2)}, u32[]{:S(2)}) collective-permute-start(f32[129,8,128]{2,1,0:T(8,128)S(1)} %maximum_maximum_fusion), channel_id=1, source_target_pairs={{0,15},{1,2},{2,1},{3,4},{4,3},{5,6},{6,5},{7,8},{8,7},{9,10},{10,... | collective-permute-start | bytes 1585160 | tf_op jit(solution)/shard_map/ppermute | solution.py:300
  7.3 0.0 copy-done.1
  7.3 0.0 copy-done.2
  7.3 0.0 copy-done.3
  7.4 1.9 %collective-permute-start.1 = (f32[128,8,128]{2,1,0:T(8,128)S(1)}, f32[128,8,128]{2,1,0:T(8,128)S(1)}, u32[]{:S(2)}, u32[]{:S(2)}) collective-permute-start(f32[128,8,128]{2,1,0:T(8,128)S(1)} %pad_maximum_fusion.own), channel_id=1, source_target_pairs={{0,1},{1,0},{2,3},{3,2},{4,5},{5,4},{6,7},{7,6},{8,9},{9,8},{10,11... | collective-permute-start | bytes 1572872 | tf_op jit(solution)/shard_map/ppermute | solution.py:299
  9.3 1.9 %collective-permute-done.1.inner = f32[128,8,128]{2,1,0:T(8,128)S(1)} collective-permute-done((f32[128,8,128]{2,1,0:T(8,128)S(1)}, f32[128,8,128]{2,1,0:T(8,128)S(1)}, u32[]{:S(2)}, u32[]{:S(2)}) %collective-permute-start.1) | collective-permute-done | bytes 524320 | tf_op jit(solution)/shard_map/ppermute | solution.py:299
  11.2 0.0 copy-start
  11.2 3.0 %near.1 = (f32[16,2,16,128]{3,2,1,0:T(8,128)S(1)}, f32[8,2048]{1,0:T(8,128)S(1)}) custom-call(s32[1]{0:T(128)} %bitcast.parity, f32[128,8,128]{2,1,0:T(8,128)S(1)} %pad_maximum_fusion.own, f32[128,8,128]{2,1,0:T(8,128)S(1)} %collective-permute-done.1.inner), custom_call_target="tpu_custom_call" | custom-call | tf_op jit(solution)/shard_map/near/pallas_call | solution.py:126
  14.2 1.9 %collective-permute-done.outer = f32[129,8,128]{2,1,0:T(8,128)S(1)} collective-permute-done((f32[129,8,128]{2,1,0:T(8,128)S(1)}, f32[129,8,128]{2,1,0:T(8,128)S(1)}, u32[]{:S(2)}, u32[]{:S(2)}) %collective-permute-start) | collective-permute-done | bytes 528416 | tf_op jit(solution)/shard_map/ppermute | solution.py:300
  16.1 0.0 copy-done
  16.1 3.3 %far.1 = (f32[16,2048]{1,0:T(8,128)S(1)}, f32[16,2048]{1,0:T(8,128)S(1)}, f32[32,8,128]{2,1,0:T(8,128)}) custom-call(s32[1]{0:T(128)} %bitcast.parity, f32[128,8,128]{2,1,0:T(8,128)S(1)} %pad_maximum_fusion.own, f32[16,2048]{1,0:T(8,128)S(1)} %copy-done, f32[129,8,128]{2,1,0:T(8,128)S(1)} %collective-permute-done.outer, ...), custom_call_target="tpu_custom_call" | custom-call | tf_op jit(solution)/shard_map/far/pallas_call | solution.py:233
  19.5 16.2 %all-to-all-start = ((f32[32,8,128]{2,1,0:T(8,128)}), f32[32,8,128]{2,1,0:T(8,128)S(1)}, u32[]{:S(2)}, u32[]{:S(2)}) async-start(f32[32,8,128]{2,1,0:T(8,128)} %get-tuple-element.9), calls=%async_computation | async-start | bytes 262144 | tf_op jit(solution)/shard_map/all_to_all | solution.py:305
  35.7 4.0 %collective-permute-start.2 = (f32[16,2048]{1,0:T(8,128)S(1)}, f32[16,2048]{1,0:T(8,128)S(1)}, u32[]{:S(2)}, u32[]{:S(2)}) collective-permute-start(f32[16,2048]{1,0:T(8,128)S(1)} %get-tuple-element.10), channel_id=1, source_target_pairs={{0,32},{16,48},{32,64},{48,80},{64,96},{80,112},{96,128},{112,144}... | collective-permute-start | bytes 393224 | tf_op jit(solution)/shard_map/ppermute | solution.py:281
  39.8 3.1 %collective-permute-start.3 = (f32[16,2048]{1,0:T(8,128)S(1)}, f32[16,2048]{1,0:T(8,128)S(1)}, u32[]{:S(2)}, u32[]{:S(2)}) collective-permute-start(f32[16,2048]{1,0:T(8,128)S(1)} %get-tuple-element.11), channel_id=1, source_target_pairs={{0,16},{16,32},{32,48},{48,64},{64,80},{80,96},{96,112},{112,128},... | collective-permute-start | bytes 393224 | tf_op jit(solution)/shard_map/ppermute | solution.py:281
  42.9 9.2 %all-to-all-done.terms = f32[32,8,128]{2,1,0:T(8,128)S(1)} async-done(((f32[32,8,128]{2,1,0:T(8,128)}), f32[32,8,128]{2,1,0:T(8,128)S(1)}, u32[]{:S(2)}, u32[]{:S(2)}) %all-to-all-start) | async-done | bytes 131104 | tf_op jit(solution)/shard_map/all_to_all | solution.py:305
  52.0 0.7 coarse_solve.1
  52.7 3.9 %all-to-all-start.1 = ((f32[32,8,128]{2,1,0:T(8,128)}), f32[32,8,128]{2,1,0:T(8,128)S(1)}, u32[]{:S(2)}, u32[]{:S(2)}) async-start(f32[32,8,128]{2,1,0:T(8,128)} %coarse_solve.1), calls=%async_computation.1 | async-start | bytes 262144 | tf_op jit(solution)/shard_map/all_to_all | solution.py:309
  56.6 0.0 collective-permute-done.2
  56.6 0.0 collective-permute-done.3
  56.6 0.7 subtract_bitcast_fusion
  57.3 14.6 %all-to-all-done.1 = f32[32,8,128]{2,1,0:T(8,128)S(1)} async-done(((f32[32,8,128]{2,1,0:T(8,128)}), f32[32,8,128]{2,1,0:T(8,128)S(1)}, u32[]{:S(2)}, u32[]{:S(2)}) %all-to-all-start.1) | async-done | bytes 131104 | tf_op jit(solution)/shard_map/all_to_all | solution.py:309
  71.8 0.7 copy.7
  (3 shorter events, 0.1 us)
Async XLA Ops:
  0.6 6.6 %copy-start.1 = (f32[2,16,2048]{2,1,0:T(8,128)S(1)}, f32[2,16,2048]{2,1,0:T(8,128)}, u32[]{:S(2)}) copy-start(f32[2,16,2048]{2,1,0:T(8,128)} %param.5) | copy-start | bytes 786436
  0.7 6.6 %copy-start.2 = (f32[16,2048]{1,0:T(8,128)S(1)}, f32[16,2048]{1,0:T(8,128)}, u32[]{:S(2)}) copy-start(f32[16,2048]{1,0:T(8,128)} %param.6) | copy-start | bytes 393220
  0.7 6.6 %copy-start.3 = (f32[1,16,2048]{2,1,0:T(8,128)S(1)}, f32[1,16,2048]{2,1,0:T(8,128)}, u32[]{:S(2)}) copy-start(f32[1,16,2048]{2,1,0:T(8,128)} %param.4) | copy-start | bytes 393220
  2.0 14.2 %collective-permute-start = (f32[129,8,128]{2,1,0:T(8,128)S(1)}, f32[129,8,128]{2,1,0:T(8,128)S(1)}, u32[]{:S(2)}, u32[]{:S(2)}) collective-permute-start(f32[129,8,128]{2,1,0:T(8,128)S(1)} %maximum_maximum_fusion), channel_id=1, source_target_pairs={{0,15},{1,2},{2,1},{3,4},{4,3},{5,6},{6,5},{7,8},{8,7},{9,10},{10,... | collective-permute-start | bytes 1585160 | tf_op jit(solution)/shard_map/ppermute | solution.py:300
  7.4 3.8 %collective-permute-start.1 = (f32[128,8,128]{2,1,0:T(8,128)S(1)}, f32[128,8,128]{2,1,0:T(8,128)S(1)}, u32[]{:S(2)}, u32[]{:S(2)}) collective-permute-start(f32[128,8,128]{2,1,0:T(8,128)S(1)} %pad_maximum_fusion.own), channel_id=1, source_target_pairs={{0,1},{1,0},{2,3},{3,2},{4,5},{5,4},{6,7},{7,6},{8,9},{9,8},{10,11... | collective-permute-start | bytes 1572872 | tf_op jit(solution)/shard_map/ppermute | solution.py:299
  11.2 5.0 %copy-start = (f32[16,2048]{1,0:T(8,128)S(1)}, f32[16,2048]{1,0:T(8,128)}, u32[]{:S(2)}) copy-start(f32[16,2048]{1,0:T(8,128)} %rate.1) | copy-start | bytes 393220
  19.5 32.5 %all-to-all-start = ((f32[32,8,128]{2,1,0:T(8,128)}), f32[32,8,128]{2,1,0:T(8,128)S(1)}, u32[]{:S(2)}, u32[]{:S(2)}) async-start(f32[32,8,128]{2,1,0:T(8,128)} %get-tuple-element.9), calls=%async_computation | async-start | bytes 262144 | tf_op jit(solution)/shard_map/all_to_all | solution.py:305
  35.7 20.9 %collective-permute-start.2 = (f32[16,2048]{1,0:T(8,128)S(1)}, f32[16,2048]{1,0:T(8,128)S(1)}, u32[]{:S(2)}, u32[]{:S(2)}) collective-permute-start(f32[16,2048]{1,0:T(8,128)S(1)} %get-tuple-element.10), channel_id=1, source_target_pairs={{0,32},{16,48},{32,64},{48,80},{64,96},{80,112},{96,128},{112,144}... | collective-permute-start | bytes 393224 | tf_op jit(solution)/shard_map/ppermute | solution.py:281
  39.8 16.8 %collective-permute-start.3 = (f32[16,2048]{1,0:T(8,128)S(1)}, f32[16,2048]{1,0:T(8,128)S(1)}, u32[]{:S(2)}, u32[]{:S(2)}) collective-permute-start(f32[16,2048]{1,0:T(8,128)S(1)} %get-tuple-element.11), channel_id=1, source_target_pairs={{0,16},{16,32},{32,48},{48,64},{64,80},{80,96},{96,112},{112,128},... | collective-permute-start | bytes 393224 | tf_op jit(solution)/shard_map/ppermute | solution.py:281
  52.7 19.1 %all-to-all-start.1 = ((f32[32,8,128]{2,1,0:T(8,128)}), f32[32,8,128]{2,1,0:T(8,128)S(1)}, u32[]{:S(2)}, u32[]{:S(2)}) async-start(f32[32,8,128]{2,1,0:T(8,128)} %coarse_solve.1), calls=%async_computation.1 | async-start | bytes 262144 | tf_op jit(solution)/shard_map/all_to_all | solution.py:309

commit v6 on v5

--- a/solution.py
+++ b/solution.py
@@ -6,6 +6,7 @@
 from jax.sharding import PartitionSpec as P
 
 M = 8
+FIRST = 11
 nonlinear_weight = 0.05
 
 
@@ -301,12 +302,15 @@
     parity = (lax.axis_index("space") % 2).reshape(1)
     history, first_half = near(parity, message, inner)
     second, first, term = far(parity, message, coarse_rate, outer, history, first_half)
-    rate = lax.dynamic_index_in_dim(to_tiles(coarse_rate), lax.axis_index("tm"), 0, keepdims=False)
-    terms = lax.all_to_all(term, "tm", 0, 0, tiled=True)
+    count = lax.axis_size("tm")
+    ring = [[(k + FIRST) % count for k in range(count)]]
+    place = (lax.axis_index("tm") + count - FIRST) % count
+    rate = lax.dynamic_index_in_dim(to_tiles(coarse_rate), place, 0, keepdims=False)
+    terms = lax.all_to_all(term, "tm", 0, 0, tiled=True, axis_index_groups=ring)
     second = passed_along(second, "tm", 2)
     first = passed_along(first, "tm", 1)
     points = coarse_solve(terms, rate)
-    points = lax.all_to_all(points, "tm", 0, 0, tiled=True)
+    points = lax.all_to_all(points, "tm", 0, 0, tiled=True, axis_index_groups=ring)
     residual = second - first
     cpoints = from_tiles(points, height, width)
     return cpoints[None], residual[None]

time: 73.8 us -> 66.4 us (0.90)
  waiting for transfers between devices: 27.5 us -> 13 us
  starting transfers between devices: 34.4 us -> 42.2 us
    all_to_all x2, waiting for transfers between devices: 23.7 us -> 9.21 us  [the longest x1 8.16 us: shards(): lax.all_to_all(points, 'tm', 0, 0, tiled=True, axis_index_groups=ring)]
    all_to_all x2, starting transfers between devices: 20.1 us -> 27.9 us  [the longest x1 16.8 us: shards(): terms = lax.all_to_all(term, 'tm', 0, 0, tiled=True, axis_index_groups=ring)]
  transfers between devices with their start and end apart: 6 -> 6, of which waited for: 4 -> 4; matrix products, arithmetic and copies ran while one was open for 1% -> 1% of each run, Pallas kernels for 5% -> 6%
where the time goes in v6:
time: 66.4 us; the launch traced here: 65.8 us
  starting transfers between devices  42.2 us (64%)
  waiting for transfers between devices  13 us (20%)
  Pallas kernels  7.07 us (11%)
  other arithmetic  2 us (3%)
  between operations  0.81 us (1%)
  local copies, waits for them, and re-layouts  0.69 us (1%)
    all_to_all x1, starting transfers between devices, shards(): terms = lax.all_to_all(term, 'tm', 0, 0, tiled=True, axis_index_groups=ring)  16.8 us
    all_to_all x1, starting transfers between devices, shards(): lax.all_to_all(points, 'tm', 0, 0, tiled=True, axis_index_groups=ring)  11.1 us
    all_to_all x1, waiting for transfers between devices, shards(): lax.all_to_all(points, 'tm', 0, 0, tiled=True, axis_index_groups=ring)  8.16 us
    ppermute x2, starting transfers between devices, passed_along(): lax.ppermute(value, axis, [(i, (i + steps) % count) for i in range(count)])  7.1 us
    ppermute x1, starting transfers between devices, shards(): lax.ppermute(jnp.concatenate(parts + [jnp.zeros((1, 8, 128), jnp.float32)...  5.3 us
    pallas_call x1, Pallas kernels, far(): pl.pallas_call(far_kernel, out_shape=(shape(height, width), shape(height,...  3.34 us
    pallas_call x1, Pallas kernels, near(): pl.pallas_call(near_kernel, out_shape=(jax.ShapeDtypeStruct((2 * M, 2, ti...  3.03 us
    ppermute x1, waiting for transfers between devices, shards(): lax.ppermute(jnp.concatenate(parts + [jnp.zeros((1, 8, 128), jnp.float32)...  1.93 us
  transfers between devices with their start and end apart: 6, of which 4 were waited for; matrix products, arithmetic and copies ran while one was open for 1% of the time, Pallas kernels for 6%

profile of v6, /device:TPU:7, one launch (start us, length us, event | category | flops | bytes accessed | tf_op | source)
XLA Modules:
  0.0 65.8 jit_solution(16527428844919892564)
XLA Ops:
  0.6 0.0 copy-start.1
  0.7 0.0 copy-start.2
  0.7 0.0 copy-start.3
  0.7 1.3 %maximum_maximum_fusion = f32[129,8,128]{2,1,0:T(8,128)S(1)} fusion(f32[32,8,128]{2,1,0:T(8,128)} %bitcast.35, f32[64,8,128]{2,1,0:T(8,128)} %bitcast.32, f32[32,8,128]{2,1,0:T(8,128)} %bitcast.37, f32[129]{0:T(256)S(1)} %pad.3.clone), kind=kLoop, calls=%fused_computation | loop fusion | flops 396288 | bytes 1053188 | tf_op jit(solution)/shard_map/concatenate | solution.py:301
  2.0 5.3 %collective-permute-start = (f32[129,8,128]{2,1,0:T(8,128)S(1)}, f32[129,8,128]{2,1,0:T(8,128)S(1)}, u32[]{:S(2)}, u32[]{:S(2)}) collective-permute-start(f32[129,8,128]{2,1,0:T(8,128)S(1)} %maximum_maximum_fusion), channel_id=1, source_target_pairs={{0,15},{1,2},{2,1},{3,4},{4,3},{5,6},{6,5},{7,8},{8,7},{9,10},{10,... | collective-permute-start | bytes 1585160 | tf_op jit(solution)/shard_map/ppermute | solution.py:301
  7.3 0.0 copy-done.1
  7.3 0.0 copy-done.2
  7.3 0.0 copy-done.3
  7.4 1.9 %collective-permute-start.1 = (f32[128,8,128]{2,1,0:T(8,128)S(1)}, f32[128,8,128]{2,1,0:T(8,128)S(1)}, u32[]{:S(2)}, u32[]{:S(2)}) collective-permute-start(f32[128,8,128]{2,1,0:T(8,128)S(1)} %pad_maximum_fusion.own), channel_id=1, source_target_pairs={{0,1},{1,0},{2,3},{3,2},{4,5},{5,4},{6,7},{7,6},{8,9},{9,8},{10,11... | collective-permute-start | bytes 1572872 | tf_op jit(solution)/shard_map/ppermute | solution.py:300
  9.3 1.9 %collective-permute-done.1.inner = f32[128,8,128]{2,1,0:T(8,128)S(1)} collective-permute-done((f32[128,8,128]{2,1,0:T(8,128)S(1)}, f32[128,8,128]{2,1,0:T(8,128)S(1)}, u32[]{:S(2)}, u32[]{:S(2)}) %collective-permute-start.1) | collective-permute-done | bytes 524320 | tf_op jit(solution)/shard_map/ppermute | solution.py:300
  11.2 0.0 copy-start
  11.2 3.0 %near.1 = (f32[16,2,16,128]{3,2,1,0:T(8,128)S(1)}, f32[8,2048]{1,0:T(8,128)S(1)}) custom-call(s32[1]{0:T(128)} %bitcast.parity, f32[128,8,128]{2,1,0:T(8,128)S(1)} %pad_maximum_fusion.own, f32[128,8,128]{2,1,0:T(8,128)S(1)} %collective-permute-done.1.inner), custom_call_target="tpu_custom_call" | custom-call | tf_op jit(solution)/shard_map/near/pallas_call | solution.py:127
  14.2 1.9 %collective-permute-done.outer = f32[129,8,128]{2,1,0:T(8,128)S(1)} collective-permute-done((f32[129,8,128]{2,1,0:T(8,128)S(1)}, f32[129,8,128]{2,1,0:T(8,128)S(1)}, u32[]{:S(2)}, u32[]{:S(2)}) %collective-permute-start) | collective-permute-done | bytes 528416 | tf_op jit(solution)/shard_map/ppermute | solution.py:301
  16.1 0.0 copy-done
  16.1 3.3 %far.1 = (f32[16,2048]{1,0:T(8,128)S(1)}, f32[16,2048]{1,0:T(8,128)S(1)}, f32[32,8,128]{2,1,0:T(8,128)}) custom-call(s32[1]{0:T(128)} %bitcast.parity, f32[128,8,128]{2,1,0:T(8,128)S(1)} %pad_maximum_fusion.own, f32[16,2048]{1,0:T(8,128)S(1)} %copy-done, f32[129,8,128]{2,1,0:T(8,128)S(1)} %collective-permute-done.outer, ...), custom_call_target="tpu_custom_call" | custom-call | tf_op jit(solution)/shard_map/far/pallas_call | solution.py:234
  19.5 16.8 %all-to-all-start = ((f32[32,8,128]{2,1,0:T(8,128)}), f32[32,8,128]{2,1,0:T(8,128)S(1)}, u32[]{:S(2)}, u32[]{:S(2)}) async-start(f32[32,8,128]{2,1,0:T(8,128)} %get-tuple-element.9), calls=%async_computation | async-start | bytes 262144 | tf_op jit(solution)/shard_map/all_to_all | solution.py:309
  36.3 4.0 %collective-permute-start.2 = (f32[16,2048]{1,0:T(8,128)S(1)}, f32[16,2048]{1,0:T(8,128)S(1)}, u32[]{:S(2)}, u32[]{:S(2)}) collective-permute-start(f32[16,2048]{1,0:T(8,128)S(1)} %get-tuple-element.10), channel_id=1, source_target_pairs={{0,32},{16,48},{32,64},{48,80},{64,96},{80,112},{96,128},{112,144}... | collective-permute-start | bytes 393224 | tf_op jit(solution)/shard_map/ppermute | solution.py:282
  40.3 3.1 %collective-permute-start.3 = (f32[16,2048]{1,0:T(8,128)S(1)}, f32[16,2048]{1,0:T(8,128)S(1)}, u32[]{:S(2)}, u32[]{:S(2)}) collective-permute-start(f32[16,2048]{1,0:T(8,128)S(1)} %get-tuple-element.11), channel_id=1, source_target_pairs={{0,16},{16,32},{32,48},{48,64},{64,80},{80,96},{96,112},{112,128},... | collective-permute-start | bytes 393224 | tf_op jit(solution)/shard_map/ppermute | solution.py:282
  43.4 1.0 %all-to-all-done.terms = f32[32,8,128]{2,1,0:T(8,128)S(1)} async-done(((f32[32,8,128]{2,1,0:T(8,128)}), f32[32,8,128]{2,1,0:T(8,128)S(1)}, u32[]{:S(2)}, u32[]{:S(2)}) %all-to-all-start) | async-done | bytes 131104 | tf_op jit(solution)/shard_map/all_to_all | solution.py:309
  44.5 0.7 %coarse_solve.1 = f32[32,8,128]{2,1,0:T(8,128)} custom-call(f32[32,8,128]{2,1,0:T(8,128)S(1)} %all-to-all-done.terms, f32[8,128]{1,0:T(8,128)S(1)} %dynamic-slice_bitcast_fusion.rate), custom_call_target="tpu_custom_call" | custom-call | tf_op jit(solution)/shard_map/coarse_solve/pallas_call | solution.py:272
  45.2 11.1 %all-to-all-start.1 = ((f32[32,8,128]{2,1,0:T(8,128)}), f32[32,8,128]{2,1,0:T(8,128)S(1)}, u32[]{:S(2)}, u32[]{:S(2)}) async-start(f32[32,8,128]{2,1,0:T(8,128)} %coarse_solve.1), calls=%async_computation.1 | async-start | bytes 262144 | tf_op jit(solution)/shard_map/all_to_all | solution.py:313
  56.3 0.0 collective-permute-done.2
  56.3 0.0 collective-permute-done.3
  56.3 0.7 %subtract_bitcast_fusion = f32[1,16,2048]{2,1,0:T(8,128)} fusion(f32[16,2048]{1,0:T(8,128)S(1)} %collective-permute-done.2, f32[16,2048]{1,0:T(8,128)S(1)} %collective-permute-done.3), kind=kLoop, calls=%fused_computation.2 | loop fusion | flops 32768 | bytes 393216 | tf_op jit(solution)/shard_map/broadcast_in_dim | solution.py:316
  56.9 8.2 %all-to-all-done.1 = f32[32,8,128]{2,1,0:T(8,128)S(1)} async-done(((f32[32,8,128]{2,1,0:T(8,128)}), f32[32,8,128]{2,1,0:T(8,128)S(1)}, u32[]{:S(2)}, u32[]{:S(2)}) %all-to-all-start.1) | async-done | bytes 131104 | tf_op jit(solution)/shard_map/all_to_all | solution.py:313
  65.1 0.7 copy.7
  (3 shorter events, 0.1 us)
Async XLA Ops:
  0.6 6.6 %copy-start.1 = (f32[2,16,2048]{2,1,0:T(8,128)S(1)}, f32[2,16,2048]{2,1,0:T(8,128)}, u32[]{:S(2)}) copy-start(f32[2,16,2048]{2,1,0:T(8,128)} %param.5) | copy-start | bytes 786436
  0.7 6.6 %copy-start.2 = (f32[16,2048]{1,0:T(8,128)S(1)}, f32[16,2048]{1,0:T(8,128)}, u32[]{:S(2)}) copy-start(f32[16,2048]{1,0:T(8,128)} %param.6) | copy-start | bytes 393220
  0.7 6.6 %copy-start.3 = (f32[1,16,2048]{2,1,0:T(8,128)S(1)}, f32[1,16,2048]{2,1,0:T(8,128)}, u32[]{:S(2)}) copy-start(f32[1,16,2048]{2,1,0:T(8,128)} %param.4) | copy-start | bytes 393220
  2.0 14.2 %collective-permute-start = (f32[129,8,128]{2,1,0:T(8,128)S(1)}, f32[129,8,128]{2,1,0:T(8,128)S(1)}, u32[]{:S(2)}, u32[]{:S(2)}) collective-permute-start(f32[129,8,128]{2,1,0:T(8,128)S(1)} %maximum_maximum_fusion), channel_id=1, source_target_pairs={{0,15},{1,2},{2,1},{3,4},{4,3},{5,6},{6,5},{7,8},{8,7},{9,10},{10,... | collective-permute-start | bytes 1585160 | tf_op jit(solution)/shard_map/ppermute | solution.py:301
  7.4 3.8 %collective-permute-start.1 = (f32[128,8,128]{2,1,0:T(8,128)S(1)}, f32[128,8,128]{2,1,0:T(8,128)S(1)}, u32[]{:S(2)}, u32[]{:S(2)}) collective-permute-start(f32[128,8,128]{2,1,0:T(8,128)S(1)} %pad_maximum_fusion.own), channel_id=1, source_target_pairs={{0,1},{1,0},{2,3},{3,2},{4,5},{5,4},{6,7},{7,6},{8,9},{9,8},{10,11... | collective-permute-start | bytes 1572872 | tf_op jit(solution)/shard_map/ppermute | solution.py:300
  11.2 5.0 %copy-start = (f32[16,2048]{1,0:T(8,128)S(1)}, f32[16,2048]{1,0:T(8,128)}, u32[]{:S(2)}) copy-start(f32[16,2048]{1,0:T(8,128)} %rate.1) | copy-start | bytes 393220
  19.5 25.0 %all-to-all-start = ((f32[32,8,128]{2,1,0:T(8,128)}), f32[32,8,128]{2,1,0:T(8,128)S(1)}, u32[]{:S(2)}, u32[]{:S(2)}) async-start(f32[32,8,128]{2,1,0:T(8,128)} %get-tuple-element.9), calls=%async_computation | async-start | bytes 262144 | tf_op jit(solution)/shard_map/all_to_all | solution.py:309
  36.3 20.0 %collective-permute-start.2 = (f32[16,2048]{1,0:T(8,128)S(1)}, f32[16,2048]{1,0:T(8,128)S(1)}, u32[]{:S(2)}, u32[]{:S(2)}) collective-permute-start(f32[16,2048]{1,0:T(8,128)S(1)} %get-tuple-element.10), channel_id=1, source_target_pairs={{0,32},{16,48},{32,64},{48,80},{64,96},{80,112},{96,128},{112,144}... | collective-permute-start | bytes 393224 | tf_op jit(solution)/shard_map/ppermute | solution.py:282
  40.3 16.0 %collective-permute-start.3 = (f32[16,2048]{1,0:T(8,128)S(1)}, f32[16,2048]{1,0:T(8,128)S(1)}, u32[]{:S(2)}, u32[]{:S(2)}) collective-permute-start(f32[16,2048]{1,0:T(8,128)S(1)} %get-tuple-element.11), channel_id=1, source_target_pairs={{0,16},{16,32},{32,48},{48,64},{64,80},{80,96},{96,112},{112,128},... | collective-permute-start | bytes 393224 | tf_op jit(solution)/shard_map/ppermute | solution.py:282
  45.2 20.0 %all-to-all-start.1 = ((f32[32,8,128]{2,1,0:T(8,128)}), f32[32,8,128]{2,1,0:T(8,128)S(1)}, u32[]{:S(2)}, u32[]{:S(2)}) async-start(f32[32,8,128]{2,1,0:T(8,128)} %coarse_solve.1), calls=%async_computation.1 | async-start | bytes 262144 | tf_op jit(solution)/shard_map/all_to_all | solution.py:313

commit v7 on v6

--- a/solution.py
+++ b/solution.py
@@ -131,8 +131,8 @@
             jax.ShapeDtypeStruct((M, width), jnp.float32),
         ),
         scratch_shapes=[
-            pltpu.VMEM((tiles, 2 * height, 128), jnp.float32),
-            pltpu.VMEM((4, tiles, 2 * height, 128), jnp.float32),
+            pltpu.VMEM((tiles, 2 * height + 8, 128), jnp.float32),
+            pltpu.VMEM((4, tiles, 2 * height + 8, 128), jnp.float32),
             pltpu.VMEM((tiles, 4, 8, 128), jnp.float32),
             pltpu.VMEM((tiles, 4, 8, 128), jnp.float32),
             pltpu.VMEM((4, tiles, 4, 8, 128), jnp.float32),
@@ -221,7 +221,7 @@
     unfold()
     for c in range(tiles):
         cols = slice(c * 128, c * 128 + 128)
-        second_out[:, cols] = rows[c]
+        second_out[:, cols] = rows[c, 0 : 2 * M]
         for r in range(2):
             part = (slice(r * 8, r * 8 + 8), cols)
             term_out[r * tiles + c] = rows[c, r * 8 : r * 8 + 8] - jnp.exp(-rate[part]) * first_out[part]
@@ -235,8 +235,8 @@
         far_kernel,
         out_shape=(shape(height, width), shape(height, width), shape(2 * tiles, 8, 128)),
         scratch_shapes=[
-            pltpu.VMEM((tiles, height, 128), jnp.float32),
-            pltpu.VMEM((4, tiles, 2 * height, 128), jnp.float32),
+            pltpu.VMEM((tiles, height + 8, 128), jnp.float32),
+            pltpu.VMEM((4, tiles, 2 * height + 8, 128), jnp.float32),
             pltpu.VMEM((tiles, 2, 8, 128), jnp.float32),
             pltpu.VMEM((tiles, 2, 8, 128), jnp.float32),
         ],

time: 66.4 us -> 66.5 us (level)
  no operation moved by 1% of the time
where the time goes in v7:
time: 66.5 us; the launch traced here: 65.8 us
  starting transfers between devices  42.2 us (63%)
  waiting for transfers between devices  13 us (20%)
  Pallas kernels  7.06 us (11%)
  other arithmetic  2 us (3%)
  between operations  0.81 us (1%)
  local copies, waits for them, and re-layouts  0.69 us (1%)
    all_to_all x1, starting transfers between devices, shards(): terms = lax.all_to_all(term, 'tm', 0, 0, tiled=True, axis_index_groups=ring)  16.8 us
    all_to_all x1, starting transfers between devices, shards(): lax.all_to_all(points, 'tm', 0, 0, tiled=True, axis_index_groups=ring)  11.1 us
    all_to_all x1, waiting for transfers between devices, shards(): lax.all_to_all(points, 'tm', 0, 0, tiled=True, axis_index_groups=ring)  8.17 us
    ppermute x2, starting transfers between devices, passed_along(): lax.ppermute(value, axis, [(i, (i + steps) % count) for i in range(count)])  7.1 us
    ppermute x1, starting transfers between devices, shards(): lax.ppermute(jnp.concatenate(parts + [jnp.zeros((1, 8, 128), jnp.float32)...  5.3 us
    pallas_call x1, Pallas kernels, far(): pl.pallas_call(far_kernel, out_shape=(shape(height, width), shape(height,...  3.34 us
    pallas_call x1, Pallas kernels, near(): pl.pallas_call(near_kernel, out_shape=(jax.ShapeDtypeStruct((2 * M, 2, ti...  3.03 us
    ppermute x1, waiting for transfers between devices, shards(): lax.ppermute(jnp.concatenate(parts + [jnp.zeros((1, 8, 128), jnp.float32)...  1.94 us
  transfers between devices with their start and end apart: 6, of which 4 were waited for; matrix products, arithmetic and copies ran while one was open for 1% of the time, Pallas kernels for 6%

profile of v7, /device:TPU:7, one launch (start us, length us, event | category | flops | bytes accessed | tf_op | source)
XLA Modules:
  0.0 65.8 jit_solution(12584986257397639838)
XLA Ops:
  0.6 0.0 copy-start.1
  0.7 0.0 copy-start.2
  0.7 0.0 copy-start.3
  0.7 1.3 %maximum_maximum_fusion = f32[129,8,128]{2,1,0:T(8,128)S(1)} fusion(f32[32,8,128]{2,1,0:T(8,128)} %bitcast.35, f32[64,8,128]{2,1,0:T(8,128)} %bitcast.32, f32[32,8,128]{2,1,0:T(8,128)} %bitcast.37, f32[129]{0:T(256)S(1)} %pad.3.clone), kind=kLoop, calls=%fused_computation | loop fusion | flops 396288 | bytes 1053188 | tf_op jit(solution)/shard_map/concatenate | solution.py:301
  2.0 5.3 %collective-permute-start = (f32[129,8,128]{2,1,0:T(8,128)S(1)}, f32[129,8,128]{2,1,0:T(8,128)S(1)}, u32[]{:S(2)}, u32[]{:S(2)}) collective-permute-start(f32[129,8,128]{2,1,0:T(8,128)S(1)} %maximum_maximum_fusion), channel_id=1, source_target_pairs={{0,15},{1,2},{2,1},{3,4},{4,3},{5,6},{6,5},{7,8},{8,7},{9,10},{10,... | collective-permute-start | bytes 1585160 | tf_op jit(solution)/shard_map/ppermute | solution.py:301
  7.3 0.0 copy-done.1
  7.3 0.0 copy-done.2
  7.3 0.0 copy-done.3
  7.4 1.9 %collective-permute-start.1 = (f32[128,8,128]{2,1,0:T(8,128)S(1)}, f32[128,8,128]{2,1,0:T(8,128)S(1)}, u32[]{:S(2)}, u32[]{:S(2)}) collective-permute-start(f32[128,8,128]{2,1,0:T(8,128)S(1)} %pad_maximum_fusion.own), channel_id=1, source_target_pairs={{0,1},{1,0},{2,3},{3,2},{4,5},{5,4},{6,7},{7,6},{8,9},{9,8},{10,11... | collective-permute-start | bytes 1572872 | tf_op jit(solution)/shard_map/ppermute | solution.py:300
  9.3 1.9 %collective-permute-done.1.inner = f32[128,8,128]{2,1,0:T(8,128)S(1)} collective-permute-done((f32[128,8,128]{2,1,0:T(8,128)S(1)}, f32[128,8,128]{2,1,0:T(8,128)S(1)}, u32[]{:S(2)}, u32[]{:S(2)}) %collective-permute-start.1) | collective-permute-done | bytes 524320 | tf_op jit(solution)/shard_map/ppermute | solution.py:300
  11.2 0.0 copy-start
  11.2 3.0 %near.1 = (f32[16,2,16,128]{3,2,1,0:T(8,128)S(1)}, f32[8,2048]{1,0:T(8,128)S(1)}) custom-call(s32[1]{0:T(128)} %bitcast.parity, f32[128,8,128]{2,1,0:T(8,128)S(1)} %pad_maximum_fusion.own, f32[128,8,128]{2,1,0:T(8,128)S(1)} %collective-permute-done.1.inner), custom_call_target="tpu_custom_call" | custom-call | tf_op jit(solution)/shard_map/near/pallas_call | solution.py:127
  14.2 1.9 %collective-permute-done.outer = f32[129,8,128]{2,1,0:T(8,128)S(1)} collective-permute-done((f32[129,8,128]{2,1,0:T(8,128)S(1)}, f32[129,8,128]{2,1,0:T(8,128)S(1)}, u32[]{:S(2)}, u32[]{:S(2)}) %collective-permute-start) | collective-permute-done | bytes 528416 | tf_op jit(solution)/shard_map/ppermute | solution.py:301
  16.1 0.0 copy-done
  16.1 3.3 %far.1 = (f32[16,2048]{1,0:T(8,128)S(1)}, f32[16,2048]{1,0:T(8,128)S(1)}, f32[32,8,128]{2,1,0:T(8,128)}) custom-call(s32[1]{0:T(128)} %bitcast.parity, f32[128,8,128]{2,1,0:T(8,128)S(1)} %pad_maximum_fusion.own, f32[16,2048]{1,0:T(8,128)S(1)} %copy-done, f32[129,8,128]{2,1,0:T(8,128)S(1)} %collective-permute-done.outer, ...), custom_call_target="tpu_custom_call" | custom-call | tf_op jit(solution)/shard_map/far/pallas_call | solution.py:234
  19.5 16.8 %all-to-all-start = ((f32[32,8,128]{2,1,0:T(8,128)}), f32[32,8,128]{2,1,0:T(8,128)S(1)}, u32[]{:S(2)}, u32[]{:S(2)}) async-start(f32[32,8,128]{2,1,0:T(8,128)} %get-tuple-element.9), calls=%async_computation | async-start | bytes 262144 | tf_op jit(solution)/shard_map/all_to_all | solution.py:309
  36.3 4.0 %collective-permute-start.2 = (f32[16,2048]{1,0:T(8,128)S(1)}, f32[16,2048]{1,0:T(8,128)S(1)}, u32[]{:S(2)}, u32[]{:S(2)}) collective-permute-start(f32[16,2048]{1,0:T(8,128)S(1)} %get-tuple-element.10), channel_id=1, source_target_pairs={{0,32},{16,48},{32,64},{48,80},{64,96},{80,112},{96,128},{112,144}... | collective-permute-start | bytes 393224 | tf_op jit(solution)/shard_map/ppermute | solution.py:282
  40.3 3.1 %collective-permute-start.3 = (f32[16,2048]{1,0:T(8,128)S(1)}, f32[16,2048]{1,0:T(8,128)S(1)}, u32[]{:S(2)}, u32[]{:S(2)}) collective-permute-start(f32[16,2048]{1,0:T(8,128)S(1)} %get-tuple-element.11), channel_id=1, source_target_pairs={{0,16},{16,32},{32,48},{48,64},{64,80},{80,96},{96,112},{112,128},... | collective-permute-start | bytes 393224 | tf_op jit(solution)/shard_map/ppermute | solution.py:282
  43.4 1.1 %all-to-all-done.terms = f32[32,8,128]{2,1,0:T(8,128)S(1)} async-done(((f32[32,8,128]{2,1,0:T(8,128)}), f32[32,8,128]{2,1,0:T(8,128)S(1)}, u32[]{:S(2)}, u32[]{:S(2)}) %all-to-all-start) | async-done | bytes 131104 | tf_op jit(solution)/shard_map/all_to_all | solution.py:309
  44.5 0.7 %coarse_solve.1 = f32[32,8,128]{2,1,0:T(8,128)} custom-call(f32[32,8,128]{2,1,0:T(8,128)S(1)} %all-to-all-done.terms, f32[8,128]{1,0:T(8,128)S(1)} %dynamic-slice_bitcast_fusion.rate), custom_call_target="tpu_custom_call" | custom-call | tf_op jit(solution)/shard_map/coarse_solve/pallas_call | solution.py:272
  45.2 11.1 %all-to-all-start.1 = ((f32[32,8,128]{2,1,0:T(8,128)}), f32[32,8,128]{2,1,0:T(8,128)S(1)}, u32[]{:S(2)}, u32[]{:S(2)}) async-start(f32[32,8,128]{2,1,0:T(8,128)} %coarse_solve.1), calls=%async_computation.1 | async-start | bytes 262144 | tf_op jit(solution)/shard_map/all_to_all | solution.py:313
  56.3 0.0 collective-permute-done.2
  56.3 0.0 collective-permute-done.3
  56.3 0.7 %subtract_bitcast_fusion = f32[1,16,2048]{2,1,0:T(8,128)} fusion(f32[16,2048]{1,0:T(8,128)S(1)} %collective-permute-done.2, f32[16,2048]{1,0:T(8,128)S(1)} %collective-permute-done.3), kind=kLoop, calls=%fused_computation.2 | loop fusion | flops 32768 | bytes 393216 | tf_op jit(solution)/shard_map/broadcast_in_dim | solution.py:316
  57.0 8.2 %all-to-all-done.1 = f32[32,8,128]{2,1,0:T(8,128)S(1)} async-done(((f32[32,8,128]{2,1,0:T(8,128)}), f32[32,8,128]{2,1,0:T(8,128)S(1)}, u32[]{:S(2)}, u32[]{:S(2)}) %all-to-all-start.1) | async-done | bytes 131104 | tf_op jit(solution)/shard_map/all_to_all | solution.py:313
  65.1 0.7 copy.7
  (3 shorter events, 0.1 us)
Async XLA Ops:
  0.6 6.6 %copy-start.1 = (f32[2,16,2048]{2,1,0:T(8,128)S(1)}, f32[2,16,2048]{2,1,0:T(8,128)}, u32[]{:S(2)}) copy-start(f32[2,16,2048]{2,1,0:T(8,128)} %param.5) | copy-start | bytes 786436
  0.7 6.6 %copy-start.2 = (f32[16,2048]{1,0:T(8,128)S(1)}, f32[16,2048]{1,0:T(8,128)}, u32[]{:S(2)}) copy-start(f32[16,2048]{1,0:T(8,128)} %param.6) | copy-start | bytes 393220
  0.7 6.6 %copy-start.3 = (f32[1,16,2048]{2,1,0:T(8,128)S(1)}, f32[1,16,2048]{2,1,0:T(8,128)}, u32[]{:S(2)}) copy-start(f32[1,16,2048]{2,1,0:T(8,128)} %param.4) | copy-start | bytes 393220
  2.0 14.2 %collective-permute-start = (f32[129,8,128]{2,1,0:T(8,128)S(1)}, f32[129,8,128]{2,1,0:T(8,128)S(1)}, u32[]{:S(2)}, u32[]{:S(2)}) collective-permute-start(f32[129,8,128]{2,1,0:T(8,128)S(1)} %maximum_maximum_fusion), channel_id=1, source_target_pairs={{0,15},{1,2},{2,1},{3,4},{4,3},{5,6},{6,5},{7,8},{8,7},{9,10},{10,... | collective-permute-start | bytes 1585160 | tf_op jit(solution)/shard_map/ppermute | solution.py:301
  7.4 3.8 %collective-permute-start.1 = (f32[128,8,128]{2,1,0:T(8,128)S(1)}, f32[128,8,128]{2,1,0:T(8,128)S(1)}, u32[]{:S(2)}, u32[]{:S(2)}) collective-permute-start(f32[128,8,128]{2,1,0:T(8,128)S(1)} %pad_maximum_fusion.own), channel_id=1, source_target_pairs={{0,1},{1,0},{2,3},{3,2},{4,5},{5,4},{6,7},{7,6},{8,9},{9,8},{10,11... | collective-permute-start | bytes 1572872 | tf_op jit(solution)/shard_map/ppermute | solution.py:300
  11.2 5.0 %copy-start = (f32[16,2048]{1,0:T(8,128)S(1)}, f32[16,2048]{1,0:T(8,128)}, u32[]{:S(2)}) copy-start(f32[16,2048]{1,0:T(8,128)} %rate.1) | copy-start | bytes 393220
  19.5 25.0 %all-to-all-start = ((f32[32,8,128]{2,1,0:T(8,128)}), f32[32,8,128]{2,1,0:T(8,128)S(1)}, u32[]{:S(2)}, u32[]{:S(2)}) async-start(f32[32,8,128]{2,1,0:T(8,128)} %get-tuple-element.9), calls=%async_computation | async-start | bytes 262144 | tf_op jit(solution)/shard_map/all_to_all | solution.py:309
  36.3 20.0 %collective-permute-start.2 = (f32[16,2048]{1,0:T(8,128)S(1)}, f32[16,2048]{1,0:T(8,128)S(1)}, u32[]{:S(2)}, u32[]{:S(2)}) collective-permute-start(f32[16,2048]{1,0:T(8,128)S(1)} %get-tuple-element.10), channel_id=1, source_target_pairs={{0,32},{16,48},{32,64},{48,80},{64,96},{80,112},{96,128},{112,144}... | collective-permute-start | bytes 393224 | tf_op jit(solution)/shard_map/ppermute | solution.py:282
  40.3 16.0 %collective-permute-start.3 = (f32[16,2048]{1,0:T(8,128)S(1)}, f32[16,2048]{1,0:T(8,128)S(1)}, u32[]{:S(2)}, u32[]{:S(2)}) collective-permute-start(f32[16,2048]{1,0:T(8,128)S(1)} %get-tuple-element.11), channel_id=1, source_target_pairs={{0,16},{16,32},{32,48},{48,64},{64,80},{80,96},{96,112},{112,128},... | collective-permute-start | bytes 393224 | tf_op jit(solution)/shard_map/ppermute | solution.py:282
  45.2 20.0 %all-to-all-start.1 = ((f32[32,8,128]{2,1,0:T(8,128)}), f32[32,8,128]{2,1,0:T(8,128)S(1)}, u32[]{:S(2)}, u32[]{:S(2)}) async-start(f32[32,8,128]{2,1,0:T(8,128)} %coarse_solve.1), calls=%async_computation.1 | async-start | bytes 262144 | tf_op jit(solution)/shard_map/all_to_all | solution.py:313

commit v8 on v7

--- a/solution.py
+++ b/solution.py
@@ -208,7 +208,7 @@
             one(2 * h + 1, other, state, outer_is_before)
             return carry
 
-        lax.fori_loop(0, M, pair, 0)
+        lax.fori_loop(0, M, pair, 0, unroll=True)
 
     @pl.when(parity[0] == 0)
     def _():

time: 66.5 us -> 66.3 us (level)
  no operation moved by 1% of the time
where the time goes in v8:
time: 66.3 us; the launch traced here: 65.7 us
  starting transfers between devices  42.2 us (64%)
  waiting for transfers between devices  13.2 us (20%)
  Pallas kernels  6.83 us (10%)
  other arithmetic  2 us (3%)
  between operations  0.81 us (1%)
  local copies, waits for them, and re-layouts  0.69 us (1%)
    all_to_all x1, starting transfers between devices, shards(): terms = lax.all_to_all(term, 'tm', 0, 0, tiled=True, axis_index_groups=ring)  16.8 us
    all_to_all x1, starting transfers between devices, shards(): lax.all_to_all(points, 'tm', 0, 0, tiled=True, axis_index_groups=ring)  11.1 us
    all_to_all x1, waiting for transfers between devices, shards(): lax.all_to_all(points, 'tm', 0, 0, tiled=True, axis_index_groups=ring)  8.26 us
    ppermute x2, starting transfers between devices, passed_along(): lax.ppermute(value, axis, [(i, (i + steps) % count) for i in range(count)])  7.1 us
    ppermute x1, starting transfers between devices, shards(): lax.ppermute(jnp.concatenate(parts + [jnp.zeros((1, 8, 128), jnp.float32)...  5.3 us
    pallas_call x1, Pallas kernels, far(): pl.pallas_call(far_kernel, out_shape=(shape(height, width), shape(height,...  3.11 us
    pallas_call x1, Pallas kernels, near(): pl.pallas_call(near_kernel, out_shape=(jax.ShapeDtypeStruct((2 * M, 2, ti...  3.03 us
    ppermute x1, waiting for transfers between devices, shards(): lax.ppermute(jnp.concatenate(parts + [jnp.zeros((1, 8, 128), jnp.float32)...  1.94 us
  transfers between devices with their start and end apart: 6, of which 4 were waited for; matrix products, arithmetic and copies ran while one was open for 1% of the time, Pallas kernels for 6%

profile of v8, /device:TPU:7, one launch (start us, length us, event | category | flops | bytes accessed | tf_op | source)
XLA Modules:
  0.0 65.7 jit_solution(15530721903595596775)
XLA Ops:
  0.6 0.0 copy-start.1
  0.7 0.0 copy-start.2
  0.7 0.0 copy-start.3
  0.7 1.3 %maximum_maximum_fusion = f32[129,8,128]{2,1,0:T(8,128)S(1)} fusion(f32[32,8,128]{2,1,0:T(8,128)} %bitcast.35, f32[64,8,128]{2,1,0:T(8,128)} %bitcast.32, f32[32,8,128]{2,1,0:T(8,128)} %bitcast.37, f32[129]{0:T(256)S(1)} %pad.3.clone), kind=kLoop, calls=%fused_computation | loop fusion | flops 396288 | bytes 1053188 | tf_op jit(solution)/shard_map/concatenate | solution.py:301
  2.0 5.3 %collective-permute-start = (f32[129,8,128]{2,1,0:T(8,128)S(1)}, f32[129,8,128]{2,1,0:T(8,128)S(1)}, u32[]{:S(2)}, u32[]{:S(2)}) collective-permute-start(f32[129,8,128]{2,1,0:T(8,128)S(1)} %maximum_maximum_fusion), channel_id=1, source_target_pairs={{0,15},{1,2},{2,1},{3,4},{4,3},{5,6},{6,5},{7,8},{8,7},{9,10},{10,... | collective-permute-start | bytes 1585160 | tf_op jit(solution)/shard_map/ppermute | solution.py:301
  7.3 0.0 copy-done.1
  7.3 0.0 copy-done.2
  7.3 0.0 copy-done.3
  7.4 1.9 %collective-permute-start.1 = (f32[128,8,128]{2,1,0:T(8,128)S(1)}, f32[128,8,128]{2,1,0:T(8,128)S(1)}, u32[]{:S(2)}, u32[]{:S(2)}) collective-permute-start(f32[128,8,128]{2,1,0:T(8,128)S(1)} %pad_maximum_fusion.own), channel_id=1, source_target_pairs={{0,1},{1,0},{2,3},{3,2},{4,5},{5,4},{6,7},{7,6},{8,9},{9,8},{10,11... | collective-permute-start | bytes 1572872 | tf_op jit(solution)/shard_map/ppermute | solution.py:300
  9.3 1.9 %collective-permute-done.1.inner = f32[128,8,128]{2,1,0:T(8,128)S(1)} collective-permute-done((f32[128,8,128]{2,1,0:T(8,128)S(1)}, f32[128,8,128]{2,1,0:T(8,128)S(1)}, u32[]{:S(2)}, u32[]{:S(2)}) %collective-permute-start.1) | collective-permute-done | bytes 524320 | tf_op jit(solution)/shard_map/ppermute | solution.py:300
  11.2 0.0 copy-start
  11.2 3.0 %near.1 = (f32[16,2,16,128]{3,2,1,0:T(8,128)S(1)}, f32[8,2048]{1,0:T(8,128)S(1)}) custom-call(s32[1]{0:T(128)} %bitcast.parity, f32[128,8,128]{2,1,0:T(8,128)S(1)} %pad_maximum_fusion.own, f32[128,8,128]{2,1,0:T(8,128)S(1)} %collective-permute-done.1.inner), custom_call_target="tpu_custom_call" | custom-call | tf_op jit(solution)/shard_map/near/pallas_call | solution.py:127
  14.2 1.9 %collective-permute-done.outer = f32[129,8,128]{2,1,0:T(8,128)S(1)} collective-permute-done((f32[129,8,128]{2,1,0:T(8,128)S(1)}, f32[129,8,128]{2,1,0:T(8,128)S(1)}, u32[]{:S(2)}, u32[]{:S(2)}) %collective-permute-start) | collective-permute-done | bytes 528416 | tf_op jit(solution)/shard_map/ppermute | solution.py:301
  16.1 0.0 copy-done
  16.1 3.1 %far.1 = (f32[16,2048]{1,0:T(8,128)S(1)}, f32[16,2048]{1,0:T(8,128)S(1)}, f32[32,8,128]{2,1,0:T(8,128)}) custom-call(s32[1]{0:T(128)} %bitcast.parity, f32[128,8,128]{2,1,0:T(8,128)S(1)} %pad_maximum_fusion.own, f32[16,2048]{1,0:T(8,128)S(1)} %copy-done, f32[129,8,128]{2,1,0:T(8,128)S(1)} %collective-permute-done.outer, ...), custom_call_target="tpu_custom_call" | custom-call | tf_op jit(solution)/shard_map/far/pallas_call | solution.py:234
  19.3 16.8 %all-to-all-start = ((f32[32,8,128]{2,1,0:T(8,128)}), f32[32,8,128]{2,1,0:T(8,128)S(1)}, u32[]{:S(2)}, u32[]{:S(2)}) async-start(f32[32,8,128]{2,1,0:T(8,128)} %get-tuple-element.9), calls=%async_computation | async-start | bytes 262144 | tf_op jit(solution)/shard_map/all_to_all | solution.py:309
  36.0 4.0 %collective-permute-start.2 = (f32[16,2048]{1,0:T(8,128)S(1)}, f32[16,2048]{1,0:T(8,128)S(1)}, u32[]{:S(2)}, u32[]{:S(2)}) collective-permute-start(f32[16,2048]{1,0:T(8,128)S(1)} %get-tuple-element.10), channel_id=1, source_target_pairs={{0,32},{16,48},{32,64},{48,80},{64,96},{80,112},{96,128},{112,144}... | collective-permute-start | bytes 393224 | tf_op jit(solution)/shard_map/ppermute | solution.py:282
  40.1 3.1 %collective-permute-start.3 = (f32[16,2048]{1,0:T(8,128)S(1)}, f32[16,2048]{1,0:T(8,128)S(1)}, u32[]{:S(2)}, u32[]{:S(2)}) collective-permute-start(f32[16,2048]{1,0:T(8,128)S(1)} %get-tuple-element.11), channel_id=1, source_target_pairs={{0,16},{16,32},{32,48},{48,64},{64,80},{80,96},{96,112},{112,128},... | collective-permute-start | bytes 393224 | tf_op jit(solution)/shard_map/ppermute | solution.py:282
  43.2 1.1 %all-to-all-done.terms = f32[32,8,128]{2,1,0:T(8,128)S(1)} async-done(((f32[32,8,128]{2,1,0:T(8,128)}), f32[32,8,128]{2,1,0:T(8,128)S(1)}, u32[]{:S(2)}, u32[]{:S(2)}) %all-to-all-start) | async-done | bytes 131104 | tf_op jit(solution)/shard_map/all_to_all | solution.py:309
  44.3 0.7 %coarse_solve.1 = f32[32,8,128]{2,1,0:T(8,128)} custom-call(f32[32,8,128]{2,1,0:T(8,128)S(1)} %all-to-all-done.terms, f32[8,128]{1,0:T(8,128)S(1)} %dynamic-slice_bitcast_fusion.rate), custom_call_target="tpu_custom_call" | custom-call | tf_op jit(solution)/shard_map/coarse_solve/pallas_call | solution.py:272
  45.0 11.1 %all-to-all-start.1 = ((f32[32,8,128]{2,1,0:T(8,128)}), f32[32,8,128]{2,1,0:T(8,128)S(1)}, u32[]{:S(2)}, u32[]{:S(2)}) async-start(f32[32,8,128]{2,1,0:T(8,128)} %coarse_solve.1), calls=%async_computation.1 | async-start | bytes 262144 | tf_op jit(solution)/shard_map/all_to_all | solution.py:313
  56.1 0.0 collective-permute-done.2
  56.1 0.0 collective-permute-done.3
  56.1 0.7 %subtract_bitcast_fusion = f32[1,16,2048]{2,1,0:T(8,128)} fusion(f32[16,2048]{1,0:T(8,128)S(1)} %collective-permute-done.2, f32[16,2048]{1,0:T(8,128)S(1)} %collective-permute-done.3), kind=kLoop, calls=%fused_computation.2 | loop fusion | flops 32768 | bytes 393216 | tf_op jit(solution)/shard_map/broadcast_in_dim | solution.py:316
  56.8 8.3 %all-to-all-done.1 = f32[32,8,128]{2,1,0:T(8,128)S(1)} async-done(((f32[32,8,128]{2,1,0:T(8,128)}), f32[32,8,128]{2,1,0:T(8,128)S(1)}, u32[]{:S(2)}, u32[]{:S(2)}) %all-to-all-start.1) | async-done | bytes 131104 | tf_op jit(solution)/shard_map/all_to_all | solution.py:313
  65.0 0.7 copy.7
  (3 shorter events, 0.1 us)
Async XLA Ops:
  0.6 6.6 %copy-start.1 = (f32[2,16,2048]{2,1,0:T(8,128)S(1)}, f32[2,16,2048]{2,1,0:T(8,128)}, u32[]{:S(2)}) copy-start(f32[2,16,2048]{2,1,0:T(8,128)} %param.5) | copy-start | bytes 786436
  0.7 6.6 %copy-start.2 = (f32[16,2048]{1,0:T(8,128)S(1)}, f32[16,2048]{1,0:T(8,128)}, u32[]{:S(2)}) copy-start(f32[16,2048]{1,0:T(8,128)} %param.6) | copy-start | bytes 393220
  0.7 6.6 %copy-start.3 = (f32[1,16,2048]{2,1,0:T(8,128)S(1)}, f32[1,16,2048]{2,1,0:T(8,128)}, u32[]{:S(2)}) copy-start(f32[1,16,2048]{2,1,0:T(8,128)} %param.4) | copy-start | bytes 393220
  2.0 14.2 %collective-permute-start = (f32[129,8,128]{2,1,0:T(8,128)S(1)}, f32[129,8,128]{2,1,0:T(8,128)S(1)}, u32[]{:S(2)}, u32[]{:S(2)}) collective-permute-start(f32[129,8,128]{2,1,0:T(8,128)S(1)} %maximum_maximum_fusion), channel_id=1, source_target_pairs={{0,15},{1,2},{2,1},{3,4},{4,3},{5,6},{6,5},{7,8},{8,7},{9,10},{10,... | collective-permute-start | bytes 1585160 | tf_op jit(solution)/shard_map/ppermute | solution.py:301
  7.4 3.8 %collective-permute-start.1 = (f32[128,8,128]{2,1,0:T(8,128)S(1)}, f32[128,8,128]{2,1,0:T(8,128)S(1)}, u32[]{:S(2)}, u32[]{:S(2)}) collective-permute-start(f32[128,8,128]{2,1,0:T(8,128)S(1)} %pad_maximum_fusion.own), channel_id=1, source_target_pairs={{0,1},{1,0},{2,3},{3,2},{4,5},{5,4},{6,7},{7,6},{8,9},{9,8},{10,11... | collective-permute-start | bytes 1572872 | tf_op jit(solution)/shard_map/ppermute | solution.py:300
  11.2 5.0 %copy-start = (f32[16,2048]{1,0:T(8,128)S(1)}, f32[16,2048]{1,0:T(8,128)}, u32[]{:S(2)}) copy-start(f32[16,2048]{1,0:T(8,128)} %rate.1) | copy-start | bytes 393220
  19.3 25.1 %all-to-all-start = ((f32[32,8,128]{2,1,0:T(8,128)}), f32[32,8,128]{2,1,0:T(8,128)S(1)}, u32[]{:S(2)}, u32[]{:S(2)}) async-start(f32[32,8,128]{2,1,0:T(8,128)} %get-tuple-element.9), calls=%async_computation | async-start | bytes 262144 | tf_op jit(solution)/shard_map/all_to_all | solution.py:309
  36.0 20.0 %collective-permute-start.2 = (f32[16,2048]{1,0:T(8,128)S(1)}, f32[16,2048]{1,0:T(8,128)S(1)}, u32[]{:S(2)}, u32[]{:S(2)}) collective-permute-start(f32[16,2048]{1,0:T(8,128)S(1)} %get-tuple-element.10), channel_id=1, source_target_pairs={{0,32},{16,48},{32,64},{48,80},{64,96},{80,112},{96,128},{112,144}... | collective-permute-start | bytes 393224 | tf_op jit(solution)/shard_map/ppermute | solution.py:282
  40.1 16.0 %collective-permute-start.3 = (f32[16,2048]{1,0:T(8,128)S(1)}, f32[16,2048]{1,0:T(8,128)S(1)}, u32[]{:S(2)}, u32[]{:S(2)}) collective-permute-start(f32[16,2048]{1,0:T(8,128)S(1)} %get-tuple-element.11), channel_id=1, source_target_pairs={{0,16},{16,32},{32,48},{48,64},{64,80},{80,96},{96,112},{112,128},... | collective-permute-start | bytes 393224 | tf_op jit(solution)/shard_map/ppermute | solution.py:282
  45.0 20.0 %all-to-all-start.1 = ((f32[32,8,128]{2,1,0:T(8,128)}), f32[32,8,128]{2,1,0:T(8,128)S(1)}, u32[]{:S(2)}, u32[]{:S(2)}) async-start(f32[32,8,128]{2,1,0:T(8,128)} %coarse_solve.1), calls=%async_computation.1 | async-start | bytes 262144 | tf_op jit(solution)/shard_map/all_to_all | solution.py:313
